TPU v7x, 32 devices: a whole 2x2x4 slice. The times are simulated.
32 devices in a mesh: group: 8 (over y, x, core), blk: 4 (over z).
Axes of the slice: x: 2, y: 2, z: 4, core: 2. Of those that a mesh axis runs over, the one named last changes fastest.
Arguments:
- embedding: bfloat16 [4096, 1024], P(('group', 'blk'))
- cluster: int32 [4096], P(('group', 'blk')), may hold values from 0 to 127, as said below
- doc_index: int32 [4096], P(('group', 'blk')), may hold values from 0 to 4095, each once
Outputs:
- best_cosine: float32 [4096], P(('group', 'blk'))
Inputs may be any that keep to these rules, and one draw needn't show every extreme that they name: `cluster`: cluster c is owned by group c mod 8. The 128 documents of one device send at most 32 documents to one owner group; a quarter of the groups receive exactly 32 from every device.
All inputs are finite; a program needn't handle non-finite values.
Results may differ from a plain program's by a relative error of at most 0.00067.
Values may be sent and summed in bfloat16 or wider, within the bound.
No kernel may reach another device: no remote copies, remote signals or barrier semaphores. Data moves between devices by JAX's collectives and lax.ppermute only.
A program may use at most 64 MiB of HBM per device.

v0:
```python
import jax
import jax.numpy as jnp
from jax import lax
from jax.sharding import PartitionSpec as P


def pair_best(query, q_clu, q_idx, keys, k_clu, k_idx):
    count = keys.shape[0]
    width = 512
    nblocks = count // width
    key_blocks = (
        keys.reshape(nblocks, width, keys.shape[1]),
        k_clu.reshape(nblocks, width),
        k_idx.reshape(nblocks, width),
    )

    def step(carry, blocks):
        key_unit, key_clu, key_idx = blocks
        scores = jnp.einsum("md,pd->mp", query, key_unit, preferred_element_type=jnp.float32)
        same = (key_clu[None, :] == q_clu[:, None]) & (q_clu[:, None] >= 0)
        earlier = same & (key_idx[None, :] < q_idx[:, None])
        later = same & (key_idx[None, :] > q_idx[:, None])
        row_best = jnp.maximum(
            carry, jnp.max(jnp.where(earlier, scores, jnp.float32(-1.0)), axis=1)
        )
        col_best = jnp.max(jnp.where(later, scores, jnp.float32(-1.0)), axis=0)
        return (row_best, col_best)

    start_best = jnp.full((query.shape[0],), -1.0, jnp.float32)
    row_best, col_best = lax.scan(step, start_best, key_blocks)
    return (row_best, col_best.reshape(count))


def slot_source(flat_slot, slots):
    count = flat_slot.shape[0]
    match = flat_slot[None, :] == jnp.arange(slots, dtype=jnp.int32)[:, None]
    filled = jnp.any(match, axis=1)
    source = jnp.sum(jnp.where(match, jnp.arange(count, dtype=jnp.int32)[None, :], 0), axis=1)
    return (source, filled)


def pack_rows(rows_unit, rows_clu, rows_idx, flat_slot, slots):
    source, filled = slot_source(flat_slot, slots)
    packed_unit = jnp.where(filled[:, None], rows_unit[source], jnp.zeros((), jnp.bfloat16))
    packed_clu = jnp.where(filled, rows_clu[source], -1)
    packed_idx = jnp.where(filled, rows_idx[source], 0)
    return (packed_unit, packed_clu, packed_idx)


def local(embedding, cluster, doc_index):
    groups = lax.axis_size("group")
    rows = cluster.shape[0]
    width = embedding.shape[1]
    cap = 2 * rows // groups
    wide = embedding.astype(jnp.float32)
    unit = (wide * lax.rsqrt(jnp.sum(wide * wide, axis=1, keepdims=True) + 1e-06)).astype(
        jnp.bfloat16
    )
    dest = cluster % groups
    onehot = (dest[:, None] == jnp.arange(groups, dtype=jnp.int32)[None, :]).astype(jnp.int32)
    slot = jnp.sum((jnp.cumsum(onehot, axis=0) - onehot) * onehot, axis=1)
    packed_unit, packed_clu, packed_idx = pack_rows(
        unit, cluster, doc_index, dest * cap + slot, groups * cap
    )
    send_unit = packed_unit.reshape(groups, cap, width)
    send_clu = packed_clu.reshape(groups, cap)
    send_idx = packed_idx.reshape(groups, cap)
    got_unit, got_clu, got_idx = (
        lax.all_to_all(send_unit, "group", split_axis=0, concat_axis=0, tiled=True),
        lax.all_to_all(send_clu, "group", split_axis=0, concat_axis=0, tiled=True),
        lax.all_to_all(send_idx, "group", split_axis=0, concat_axis=0, tiled=True),
    )
    members = groups * cap
    query = got_unit.reshape(members, width)
    q_clu = got_clu.reshape(members)
    q_idx = got_idx.reshape(members)
    start_best = jnp.full((members,), -1.0, jnp.float32)
    row_best, col_unused = pair_best(
        query,
        q_clu,
        q_idx,
        lax.all_gather(query, "blk", axis=0, tiled=True),
        lax.all_gather(q_clu, "blk", axis=0, tiled=True),
        lax.all_gather(q_idx, "blk", axis=0, tiled=True),
    )
    best = jnp.maximum(start_best, row_best)
    back = lax.all_to_all(
        best.reshape(groups, cap), "group", split_axis=0, concat_axis=0, tiled=True
    )
    return back.reshape(groups * cap)[dest * cap + slot]


def solution(mesh):
    return jax.shard_map(
        local,
        mesh=mesh,
        in_specs=(P(("group", "blk"), None), P(("group", "blk")), P(("group", "blk"))),
        out_specs=P(("group", "blk")),
        check_vma=False,
    )
```

profile of v0, /device:TPU:0, one launch (start us, length us, event | category | flops | bytes accessed | tf_op | source)
XLA Modules:
  0.0 95.0 jit_solution(14410880335960827231)
XLA Ops:
  6.5 0.0 copy-start
  6.5 0.0 all-gather.4.cloned.1.call-start
  6.5 0.7 and_select_fusion
  7.2 0.1 fusion.8
  7.3 0.2 reduce_window_sum.11
  7.5 0.2 select_reduce_fusion.1
  7.7 0.7 compare_select_fusion.1
  8.3 0.1 select_reduce_fusion
  8.4 0.1 fusion.7
  8.6 1.1 %fusion.5 = f32[128]{0:T(128)S(1)} fusion(bf16[128,1024]{1,0:T(8,128)(2,1)} %param.5), kind=kLoop, calls=%fused_computation.16 | loop fusion | flops 393088 | bytes 262656 | tf_op jit(solution)/shard_map/reduce_sum | solution.py:56
  9.7 1.1 %fusion.6 = bf16[128,1024]{1,0:T(8,128)(2,1)S(1)} fusion(bf16[128,1024]{1,0:T(8,128)(2,1)} %param.5, f32[128]{0:T(128)S(1)} %add_rsqrt_fusion), kind=kLoop, calls=%fused_computation.17 | loop fusion | flops 393216 | bytes 524800 | tf_op jit(solution)/shard_map/convert_element_type | solution.py:56
  10.8 0.1 broadcast_in_dim.53
  10.8 1.2 %gather_fusion.2 = bf16[256,1024]{1,0:T(8,128)(2,1)S(1)} fusion(bf16[128,1024]{1,0:T(8,128)(2,1)S(1)} %fusion.6, s32[1024]{0:T(1024)S(1)} %pad_clamp_fusion.1), kind=kCustom, calls=%fused_computation.2 | custom fusion | bytes 1049600 | tf_op jit(solution)/shard_map/gather | solution.py:44
  12.0 0.0 copy-start.1
  12.0 0.1 broadcast_select_fusion
  12.1 14.8 %all_to_all.32 = bf16[8,32,1024]{2,1,0:T(8,128)(2,1)} all-to-all(bf16[8,32,1024]{2,1,0:T(8,128)(2,1)S(1)} %broadcast_select_fusion), channel_id=1, replica_groups=mesh['group'=8,'blk'=4] {'group'}, dimensions={0} | all-to-all | bytes 1048576 | tf_op jit(solution)/shard_map/all_to_all | solution.py:69
  27.0 0.0 all-gather.4.cloned.1.call-update
  27.0 0.0 copy-done.1
  27.0 1.9 %gather_fusion = s32[256]{0:T(256)S(1)} fusion(s32[128]{0:T(128)S(1)} %copy-done.1, s32[1024]{0:T(1024)S(1)} %pad_clamp_fusion.1), kind=kCustom, calls=%fused_computation | custom fusion | bytes 3072 | tf_op jit(solution)/shard_map/gather | solution.py:45
  28.9 0.0 copy-done
  28.9 1.9 %gather_fusion.1 = s32[256]{0:T(256)S(1)} fusion(s32[128]{0:T(128)S(1)} %copy-done, s32[1024]{0:T(1024)S(1)} %pad_clamp_fusion.1), kind=kCustom, calls=%fused_computation.1 | custom fusion | bytes 3072 | tf_op jit(solution)/shard_map/gather | solution.py:46
  30.8 0.7 select_n.68
  31.4 3.3 %all-to-all-start = ((s32[8,1,32]{2,1,0:T(1,128)}), s32[8,1,32]{2,1,0:T(1,128)S(1)}, u32[]{:S(2)}, u32[]{:S(2)}) async-start(s32[8,1,32]{2,1,0:T(1,128)} %select_n.68), calls=%async_computation | async-start | bytes 8192 | tf_op jit(solution)/shard_map/all_to_all | solution.py:70
  34.7 0.7 select_n.70
  35.4 3.9 %all-to-all-done = s32[8,1,32]{2,1,0:T(1,128)S(1)} async-done(((s32[8,1,32]{2,1,0:T(1,128)}), s32[8,1,32]{2,1,0:T(1,128)S(1)}, u32[]{:S(2)}, u32[]{:S(2)}) %all-to-all-start) | async-done | bytes 1056 | tf_op jit(solution)/shard_map/all_to_all | solution.py:70
  39.3 3.3 %all-to-all-start.1 = ((s32[8,1,32]{2,1,0:T(1,128)}), s32[8,1,32]{2,1,0:T(1,128)S(1)}, u32[]{:S(2)}, u32[]{:S(2)}) async-start(s32[8,1,32]{2,1,0:T(1,128)} %select_n.70), calls=%async_computation.1 | async-start | bytes 8192 | tf_op jit(solution)/shard_map/all_to_all | solution.py:71
  42.6 0.5 broadcast.121
  43.1 0.6 reduce.11
  43.7 0.1 reshape.154
  43.8 11.2 %all-gather = s32[4,1,256]{2,1,0:T(1,128)S(1)} all-gather(s32[1,1,256]{2,1,0:T(1,128)S(1)} %reshape.154), channel_id=1, replica_groups=mesh['group'=8,'blk'=4] {'blk'}, dimensions={0}, use_global_device_ids=true | all-gather | bytes 5120 | tf_op jit(solution)/shard_map/all_gather | solution.py:83
  55.0 0.0 all-to-all-done.1
  55.0 0.0 copy-start.4
  55.1 0.6 reduce.12
  55.6 0.1 reshape.156
  55.7 7.7 %all-gather.1 = s32[4,1,256]{2,1,0:T(1,128)S(1)} all-gather(s32[1,1,256]{2,1,0:T(1,128)S(1)} %reshape.156), channel_id=1, replica_groups=mesh['group'=8,'blk'=4] {'blk'}, dimensions={0}, use_global_device_ids=true | all-gather | bytes 5120 | tf_op jit(solution)/shard_map/all_gather | solution.py:84
  63.5 0.1 eq.89
  63.6 0.1 lt.59
  63.7 8.9 %all-gather.4.cloned.1.call-done = bf16[1024,1024]{1,0:T(8,128)(2,1)} async-done(((bf16[256,1024]{1,0:T(8,128)(2,1)}), bf16[1024,1024]{1,0:T(8,128)(2,1)}) %all-gather.4.cloned.1.call-update) | async-done | bytes 2097168 | tf_op jit(solution)/shard_map/all_gather | solution.py:82
  72.5 3.6 %while.12 = (s32[]{:T(128)}, f32[256]{0:T(256)S(1)}, s32[2,512]{1,0:T(2,128)S(1)}, s32[8,32]{1,0:T(8,128)}, s32[2,512]{1,0:T(2,128)S(1)}, /*index=5*/s32[8,32]{1...) while((s32[]{:T(128)}, f32[256]{0:T(256)S(1)}, ...), condition=%wide.wide.region_7.8_spmd.clone, body=%wide.wide.region_5.7_spmd.clone.sunk | while | flops 269222400 | bytes 1593475 | solution.py:30
  72.5 1.7 %fusion.19 = f32[256]{0:T(256)S(1)} fusion(bf16[256,1024]{1,0:T(8,128)(2,1)S(1)} %get-tuple-element.226, bf16[2,512,1024]{2,1,0:T(8,128)(2,1)} %get-tuple-element.225, s32[]{:T(128)} %get-tuple-element.207, s32[256]{0:T(256)S(1)} %get-tuple-element.227, s32[256]{0:T(256)S(1)} %get-tuple-element.228, s32[512]{0:T(512)S(1)} %bitcast.37, ...), kind=kOutput, calls=%fused_computation.6.clone.clone.1 | convolution fusion | flops 269221632 | bytes 1580800 | tf_op jit(solution)/shard_map/while/body/eval_jaxpr/md,pd->mp/dot_general | solution.py:19
  74.3 1.7 %fusion.19 = f32[256]{0:T(256)S(1)} fusion(bf16[256,1024]{1,0:T(8,128)(2,1)S(1)} %get-tuple-element.226, bf16[2,512,1024]{2,1,0:T(8,128)(2,1)} %get-tuple-element.225, s32[]{:T(128)} %get-tuple-element.207, s32[256]{0:T(256)S(1)} %get-tuple-element.227, s32[256]{0:T(256)S(1)} %get-tuple-element.228, s32[512]{0:T(512)S(1)} %bitcast.37, ...), kind=kOutput, calls=%fused_computation.6.clone.clone.1 | convolution fusion | flops 269221632 | bytes 1580800 | tf_op jit(solution)/shard_map/while/body/eval_jaxpr/md,pd->mp/dot_general | solution.py:19
  76.1 0.7 all_to_all.26
  76.8 3.6 %all-to-all-start.3 = ((f32[8,1,32]{2,1,0:T(1,128)}), f32[8,1,32]{2,1,0:T(1,128)S(1)}, u32[]{:S(2)}, u32[]{:S(2)}) async-start(f32[8,1,32]{2,1,0:T(1,128)} %all_to_all.26), calls=%async_computation.3 | async-start | bytes 8192 | tf_op jit(solution)/shard_map/all_to_all | solution.py:87
  80.4 4.6 %all-to-all-done.3 = f32[8,1,32]{2,1,0:T(1,128)S(1)} async-done(((f32[8,1,32]{2,1,0:T(1,128)}), f32[8,1,32]{2,1,0:T(1,128)S(1)}, u32[]{:S(2)}, u32[]{:S(2)}) %all-to-all-start.3) | async-done | bytes 1056 | tf_op jit(solution)/shard_map/all_to_all | solution.py:87
  85.1 0.5 broadcast.123
  85.6 0.7 reduce.13
  86.3 0.1 reshape.120
  86.4 1.8 %gather_fusion.3 = f32[128]{0:T(128)} fusion(f32[256]{0:T(256)S(1)} %reshape.120, s32[1024]{0:T(1024)S(1)} %pad_clamp_fusion), kind=kCustom, calls=%fused_computation.3 | custom fusion | bytes 1536 | tf_op jit(solution)/shard_map/gather | solution.py:90
  (22 shorter events, 0.2 us)
Async XLA Ops:
  6.5 22.3 %copy-start = (s32[128]{0:T(128)S(1)}, s32[128]{0:T(128)}, u32[]{:S(2)}) copy-start(s32[128]{0:T(128)} %param.7) | copy-start | bytes 1540
  6.5 66.0 %all-gather.4.cloned.1.call-start = ((), (), s32[]{:S(2)}) async-start(), calls=%async_computation.4 | async-start | bytes 2621440 | tf_op jit(solution)/shard_map/all_gather | solution.py:82
  12.0 15.0 %copy-start.1 = (s32[128]{0:T(128)S(1)}, s32[128]{0:T(128)}, u32[]{:S(2)}) copy-start(s32[128]{0:T(128)} %param.6) | copy-start | bytes 1540
  27.0 45.6 %copy-start.2 = (bf16[8,32,1024]{2,1,0:T(8,128)(2,1)S(1)}, bf16[8,32,1024]{2,1,0:T(8,128)(2,1)}, u32[]{:S(2)}) copy-start(bf16[8,32,1024]{2,1,0:T(8,128)(2,1)} %all_to_all.32) | copy-start | bytes 1572868
  31.4 7.9 %all-to-all-start = ((s32[8,1,32]{2,1,0:T(1,128)}), s32[8,1,32]{2,1,0:T(1,128)S(1)}, u32[]{:S(2)}, u32[]{:S(2)}) async-start(s32[8,1,32]{2,1,0:T(1,128)} %select_n.68), calls=%async_computation | async-start | bytes 8192 | tf_op jit(solution)/shard_map/all_to_all | solution.py:70
  39.3 33.2 %copy-start.3 = (s32[8,1,32]{2,1,0:T(1,128)}, s32[8,1,32]{2,1,0:T(1,128)S(1)}, u32[]{:S(2)}) copy-start(s32[8,1,32]{2,1,0:T(1,128)S(1)} %all-to-all-done) | copy-start | bytes 3076
  39.3 15.8 %all-to-all-start.1 = ((s32[8,1,32]{2,1,0:T(1,128)}), s32[8,1,32]{2,1,0:T(1,128)S(1)}, u32[]{:S(2)}, u32[]{:S(2)}) async-start(s32[8,1,32]{2,1,0:T(1,128)} %select_n.70), calls=%async_computation.1 | async-start | bytes 8192 | tf_op jit(solution)/shard_map/all_to_all | solution.py:71
  55.0 17.5 %copy-start.4 = (s32[8,1,32]{2,1,0:T(1,128)}, s32[8,1,32]{2,1,0:T(1,128)S(1)}, u32[]{:S(2)}) copy-start(s32[8,1,32]{2,1,0:T(1,128)S(1)} %all-to-all-done.1) | copy-start | bytes 3076
  76.8 8.3 %all-to-all-start.3 = ((f32[8,1,32]{2,1,0:T(1,128)}), f32[8,1,32]{2,1,0:T(1,128)S(1)}, u32[]{:S(2)}, u32[]{:S(2)}) async-start(f32[8,1,32]{2,1,0:T(1,128)} %all_to_all.26), calls=%async_computation.3 | async-start | bytes 8192 | tf_op jit(solution)/shard_map/all_to_all | solution.py:87
Sparse Core Ops, SparseCore 0:
  27.1 45.3 all-gather.3
where the time goes:
time: 95.5 us; the launch traced here: 95 us
  blocking collectives  33.8 us (35%)
  waiting for transfers between devices  17.4 us (18%)
  between operations  13.6 us (14%)
  local copies, waits for them, and re-layouts  10.3 us (11%)
  starting transfers between devices  10.2 us (11%)
  other arithmetic  6.19 us (6%)
  matrix products  3.46 us (4%)
    all_to_all x1, blocking collectives, local(): lax.all_to_all(send_unit, 'group', split_axis=0, concat_axis=0, tiled=True)  14.8 us
    all_gather x1, blocking collectives, local(): lax.all_gather(q_clu, 'blk', axis=0, tiled=True)  11.2 us
    all_gather x1, waiting for transfers between devices, local(): lax.all_gather(query, 'blk', axis=0, tiled=True)  8.86 us
    all_gather x1, blocking collectives, local(): lax.all_gather(q_idx, 'blk', axis=0, tiled=True)  7.74 us
    all_to_all x1, waiting for transfers between devices, local(): lax.all_to_all(best.reshape(groups, cap), 'group', split_axis=0, concat_a...  4.65 us
    all_to_all x1, waiting for transfers between devices, local(): lax.all_to_all(send_clu, 'group', split_axis=0, concat_axis=0, tiled=True)  3.9 us
    all_to_all x1, starting transfers between devices, local(): lax.all_to_all(best.reshape(groups, cap), 'group', split_axis=0, concat_a...  3.65 us
    dot_general x2, matrix products, step(): jnp.einsum('md,pd->mp', query, key_unit, preferred_element_type=jnp.float32)  3.46 us
  transfers between devices with their start and end apart: 4, of which 3 were waited for; matrix products, arithmetic and copies ran while one was open for 8% of the time, Pallas kernels for 0%

commit v1 on v0

v1 whole, which is shorter than its diff:
```python
import functools

import jax
import jax.numpy as jnp
from jax import lax
from jax.experimental import pallas as pl
from jax.experimental.pallas import tpu as pltpu
from jax.sharding import PartitionSpec as P

LANES = 128
META = 16


def pack_kernel(emb_a, clu_a, idx_a, emb_b, clu_b, idx_b, out):
    width = emb_a.shape[1]
    for half, (emb, clu, idx) in enumerate(((emb_a, clu_a, idx_a), (emb_b, clu_b, idx_b))):
        base = half * (width + META)
        wide = emb[...].astype(jnp.float32)
        norm = lax.rsqrt(jnp.sum(wide * wide, axis=1, keepdims=True) + 1e-06)
        unit = (wide * norm).astype(jnp.bfloat16)
        for k in range(width // LANES):
            out[pl.ds(base + k * LANES, LANES), :] = unit[:, k * LANES : (k + 1) * LANES]
        row = lax.broadcasted_iota(jnp.int32, (META, LANES), 0)
        index = idx[...]
        meta = jnp.where(row == 0, clu[...], jnp.where(row == 1, index >> 8, index & 255))
        out[pl.ds(base + width, META), :] = meta.astype(jnp.float32).astype(jnp.bfloat16)


def load_block(ref, base, width):
    parts = [ref[pl.ds(base + k * LANES, LANES), :] for k in range(width // LANES)]
    meta = ref[pl.ds(base + width, META), :].astype(jnp.float32)
    return jnp.concatenate(parts, axis=1), meta[0:1], meta[1:2] * 256.0 + meta[2:3]


def down(row):
    return jnp.transpose(jnp.broadcast_to(row, (LANES, LANES)))


def score_kernel(places, queries, cross, *refs):
    nkeys = 1 + max(place[0] for place in places)
    query_ref, key_refs, outs = refs[0], refs[1 : 1 + nkeys], refs[1 + nkeys :]
    step = query_ref.shape[0] // 2
    width = step - META
    loaded = [load_block(query_ref, i * step, width) for i in range(queries)]
    query = jnp.concatenate([block[0] for block in loaded], axis=0)
    q_clu = jnp.concatenate([down(block[1]) for block in loaded], axis=0)
    q_idx = jnp.concatenate([down(block[2]) for block in loaded], axis=0)
    row_best = jnp.full((queries * LANES, LANES), -1.0, jnp.float32)
    for first in range(0, len(places), 2):
        pair = places[first : first + 2]
        keys = [load_block(key_refs[place[0]], place[1] * step, width) for place in pair]
        scores = lax.dot_general(
            query,
            jnp.concatenate([key[0] for key in keys], axis=0),
            (((1,), (1,)), ((), ())),
            preferred_element_type=jnp.float32,
        )
        for number, (place, key) in enumerate(zip(pair, keys)):
            part = scores[:, number * LANES : (number + 1) * LANES]
            part = jnp.where(key[1] == q_clu, part, -1.0)
            earlier = key[2] < q_idx
            row_best = jnp.maximum(row_best, jnp.where(earlier, part, -1.0))
            if cross:
                col = jnp.max(jnp.where(earlier, -1.0, part), axis=0, keepdims=True)
                outs[1][pl.ds(place[2], 1), :] = col
    for i in range(queries):
        block = jnp.transpose(row_best[i * LANES : (i + 1) * LANES])
        outs[0][pl.ds(i, 1), :] = jnp.max(block, axis=0, keepdims=True)


def score(places, queries, query, keys, cross):
    blocks = len(places)
    width = query.shape[0] // 2 - META
    shapes = [jax.ShapeDtypeStruct((queries, LANES), jnp.float32)]
    if cross:
        shapes.append(jax.ShapeDtypeStruct((blocks, LANES), jnp.float32))
    return pl.pallas_call(
        functools.partial(score_kernel, places, queries, cross),
        out_shape=shapes,
        in_specs=[pl.BlockSpec(memory_space=pltpu.VMEM)] * (1 + len(keys)),
        out_specs=[pl.BlockSpec(memory_space=pltpu.VMEM)] * len(shapes),
        compiler_params=pltpu.CompilerParams(vmem_limit_bytes=32 * 2**20),
        cost_estimate=pl.CostEstimate(
            flops=2 * queries * blocks * LANES * LANES * width,
            bytes_accessed=2 * (queries + blocks) * LANES * width,
            transcendentals=0,
        ),
    )(query, *keys)


def program(groups, blks, embedding, cluster, doc_index):
    rows, width = embedding.shape

    def swap(x):
        return lax.ppermute(x, "group", [(g, g ^ 1) for g in range(groups)])

    def turn(x, even, odd):
        return lax.ppermute(x, "group", [(g, g ^ (odd if g & 1 else even)) for g in range(groups)])

    order = [i // 2 if i % 2 == 0 else blks - 1 - i // 2 for i in range(blks)]
    rounds = max(1, blks // 4)

    def visit(x, number, back):
        pairs = []
        for g in range(groups):
            shift = number + 1 + (rounds if g & 1 else 0)
            for i in range(blks):
                a, b = order[i], order[(i + shift) % blks]
                a, b = g * blks + a, g * blks + b
                pairs.append((b, a) if back else (a, b))
        return lax.ppermute(x, ("group", "blk"), pairs)

    clu, idx = cluster.reshape(1, rows), doc_index.reshape(1, rows)
    pair = pl.pallas_call(
        pack_kernel,
        out_shape=jax.ShapeDtypeStruct((2 * (width + META), LANES), jnp.bfloat16),
        in_specs=[pl.BlockSpec(memory_space=pltpu.VMEM)] * 6,
        out_specs=pl.BlockSpec(memory_space=pltpu.VMEM),
        compiler_params=pltpu.CompilerParams(vmem_limit_bytes=16 * 2**20),
    )(
        embedding,
        clu,
        idx,
        swap(embedding),
        swap(cluster).reshape(1, rows),
        swap(doc_index).reshape(1, rows),
    )
    step = width + META

    near = turn(pair, 2, 4)
    visitors = [visit(pair, number, False) for number in range(rounds)]
    far = turn(near[:step], 4, 2)
    near_other = swap(near)
    far_other = swap(far)
    keys = [pair, near, near_other, far, far_other]
    places = [(0, 0, 0), (0, 1, 1), (1, 0, 2), (1, 1, 3), (2, 1, 4), (2, 0, 5), (3, 0, 6), (4, 0, 7)]
    bit = 8
    while bit < groups:
        places = places + [(a + len(keys), b, p + bit) for a, b, p in places]
        keys = keys + [lax.ppermute(k, "group", [(g, g ^ bit) for g in range(groups)]) for k in keys]
        bit *= 2

    (own_best,) = score(places, 1, pair, keys, False)
    rows_back, cols = [], None
    for number, visitor in enumerate(visitors):
        row_best, col_best = score(places, 2, visitor, keys, True)
        rows_back.append(row_best)
        cols = col_best if cols is None else jnp.maximum(cols, col_best)

    bit = groups // 2
    while bit > 1:
        even, odd = bit, {2: 4, 4: 2}.get(bit, bit)
        cols = jnp.maximum(cols[:bit], turn(cols[bit:], even, odd))
        bit //= 2
    chip = cols
    for number, row_best in enumerate(rows_back):
        chip = jnp.maximum(chip, visit(row_best, number, True))
    other = swap(chip[1])
    return jnp.maximum(jnp.maximum(own_best[0], chip[0]), other)


def solution(mesh):
    return jax.shard_map(
        functools.partial(program, mesh.shape["group"], mesh.shape["blk"]),
        mesh=mesh,
        in_specs=(P(("group", "blk"), None), P(("group", "blk")), P(("group", "blk"))),
        out_specs=P(("group", "blk")),
        check_vma=False,
    )
```

time: 95.5 us -> 33 us (0.35)
  blocking collectives: 33.8 us -> 0 us
  between operations: 13.6 us -> 0.06 us
  local copies, waits for them, and re-layouts: 10.3 us -> 1.66 us
  other arithmetic: 6.19 us -> 0.52 us
  starting transfers between devices: 10.2 us -> 15.8 us
  waiting for transfers between devices: 17.4 us -> 12.8 us
  matrix products: 3.46 us -> 0 us
  Pallas kernels: 0 us -> 1.99 us
    all_gather x2 -> x0, blocking collectives: 19 us -> none  [the longest x1 11.2 us: local(): lax.all_gather(q_clu, 'blk', axis=0, tiled=True)]
    ppermute x0 -> x12, starting transfers between devices: none -> 15.8 us  [the longest x4 8.7 us: turn(): lax.ppermute(x, 'group', [(g, g ^ (odd if g & 1 else even)) for g in rang...]
    all_to_all x1 -> x0, blocking collectives: 14.8 us -> none  [local(): lax.all_to_all(send_unit, 'group', split_axis=0, concat_axis=0, tiled=True)]
    ppermute x0 -> x12, waiting for transfers between devices: none -> 12.8 us  [the longest x4 8.81 us: turn(): lax.ppermute(x, 'group', [(g, g ^ (odd if g & 1 else even)) for g in rang...]
    all_to_all x3 -> x0, starting transfers between devices: 10.2 us -> none  [the longest x1 3.65 us: local(): lax.all_to_all(best.reshape(groups, cap), 'group', split_axis=0, concat_a...]
    all_gather x1 -> x0, waiting for transfers between devices: 8.86 us -> none  [local(): lax.all_gather(query, 'blk', axis=0, tiled=True)]
    all_to_all x3 -> x0, waiting for transfers between devices: 8.55 us -> none  [the longest x1 4.65 us: local(): lax.all_to_all(best.reshape(groups, cap), 'group', split_axis=0, concat_a...]
    gather x4 -> x0, local copies, waits for them, and re-layouts: 6.67 us -> none  [the longest x1 1.87 us: pack_rows(): packed_clu = jnp.where(filled, rows_clu[source], -1)]
  transfers between devices with their start and end apart: 4 -> 12, of which waited for: 3 -> 9; matrix products, arithmetic and copies ran while one was open for 8% -> 0% of each run, Pallas kernels for 0% -> 3%
where the time goes in v1:
time: 33 us; the launch traced here: 32.9 us
  starting transfers between devices  15.8 us (48%)
  waiting for transfers between devices  12.8 us (39%)
  Pallas kernels  1.99 us (6%)
  local copies, waits for them, and re-layouts  1.66 us (5%)
  other arithmetic  0.52 us (2%)
    ppermute x4, waiting for transfers between devices, turn(): lax.ppermute(x, 'group', [(g, g ^ (odd if g & 1 else even)) for g in rang...  8.81 us
    ppermute x4, starting transfers between devices, turn(): lax.ppermute(x, 'group', [(g, g ^ (odd if g & 1 else even)) for g in rang...  8.7 us
    ppermute x2, starting transfers between devices, visit(): return lax.ppermute(x, ('group', 'blk'), pairs)  6.09 us
    ppermute x2, waiting for transfers between devices, visit(): return lax.ppermute(x, ('group', 'blk'), pairs)  2.48 us
    pallas_call x2, Pallas kernels, score(): pl.pallas_call(functools.partial(score_kernel, places, queries, cross), o...  1.81 us
    unnamed x6, local copies, waits for them, and re-layouts  1.62 us
    ppermute x6, waiting for transfers between devices, swap(): return lax.ppermute(x, 'group', [(g, g ^ 1) for g in range(groups)])  1.52 us
    ppermute x6, starting transfers between devices, swap(): return lax.ppermute(x, 'group', [(g, g ^ 1) for g in range(groups)])  1.03 us
  transfers between devices with their start and end apart: 12, of which 9 were waited for; matrix products, arithmetic and copies ran while one was open for 0% of the time, Pallas kernels for 3%

profile of v1, /device:TPU:0, one launch (start us, length us, event | category | flops | bytes accessed | tf_op | source)
XLA Modules:
  0.0 32.9 jit_solution(539152519601038757)
XLA Ops:
  0.0 0.5 %collective-permute-start = (bf16[128,1024]{1,0:T(8,128)(2,1)}, bf16[128,1024]{1,0:T(8,128)(2,1)S(1)}, u32[]{:S(2)}, u32[]{:S(2)}) collective-permute-start(bf16[128,1024]{1,0:T(8,128)(2,1)} %emb_a.1), channel_id=1, source_target_pairs={{0,4},{4,0},{8,12},{12,8},{16,20},{20,16},{24,28},{28,24},{1,5},{5... | collective-permute-start | bytes 786440 | tf_op jit(solution)/shard_map/ppermute | solution.py:95
  0.5 0.1 collective-permute-start.1
  0.5 0.5 %collective-permute-start.2 = (s32[128]{0:T(128)}, s32[128]{0:T(128)S(1)}, u32[]{:S(2)}, u32[]{:S(2)}) collective-permute-start(s32[128]{0:T(128)} %param.5), channel_id=1, source_target_pairs={{0,4},{4,0},{8,12},{12,8},{16,20},{20,16},{24,28},{28,24},{1,5},{5... | collective-permute-start | bytes 1544 | tf_op jit(solution)/shard_map/ppermute | solution.py:95
  1.0 0.9 %collective-permute-done.1 = s32[128]{0:T(128)S(1)} collective-permute-done((s32[128]{0:T(128)}, s32[128]{0:T(128)S(1)}, u32[]{:S(2)}, u32[]{:S(2)}) %collective-permute-start.1) | collective-permute-done | bytes 544 | tf_op jit(solution)/shard_map/ppermute | solution.py:95
  1.8 0.1 collective-permute-done.2
  1.9 0.0 collective-permute-done.emb_b
  1.9 0.0 copy-start.1
  1.9 0.0 copy-start.2
  1.9 0.7 %copy-done.1 = s32[128]{0:T(128)S(1)} copy-done((s32[128]{0:T(128)S(1)}, s32[128]{0:T(128)}, u32[]{:S(2)}) %copy-start.1) | copy-done | bytes 536
  2.6 0.0 copy-done.2
  2.6 0.0 copy-start
  2.6 0.9 %copy-done = bf16[128,1024]{1,0:T(8,128)(2,1)S(1)} copy-done((bf16[128,1024]{1,0:T(8,128)(2,1)S(1)}, bf16[128,1024]{1,0:T(8,128)(2,1)}, u32[]{:S(2)}) %copy-start) | copy-done | bytes 262168
  3.5 0.2 shard_map.37.refs_0_.refs_1_
  3.7 2.9 %collective-permute-start.3 = (bf16[2080,128]{1,0:T(8,128)(2,1)S(1)}, bf16[2080,128]{1,0:T(8,128)(2,1)S(1)}, u32[]{:S(2)}, u32[]{:S(2)}) collective-permute-start(bf16[2080,128]{1,0:T(8,128)(2,1)S(1)} %shard_map.37.refs_0_.refs_1_), channel_id=1, source_target_pairs={{0,8},{4,20},{8,0},{12,28},{16,24},{20,4},{24,16},{28,12},{1,9},{5... | collective-permute-start | bytes 1597448 | tf_op jit(solution)/shard_map/ppermute | solution.py:98
  6.6 3.6 %collective-permute-start.7 = (bf16[2080,128]{1,0:T(8,128)(2,1)S(1)}, bf16[2080,128]{1,0:T(8,128)(2,1)S(1)}, u32[]{:S(2)}, u32[]{:S(2)}) collective-permute-start(bf16[2080,128]{1,0:T(8,128)(2,1)S(1)} %shard_map.37.refs_0_.refs_1_), channel_id=1, source_target_pairs={{0,3},{3,1},{1,2},{2,0},{4,5},{7,6},{5,4},{6,7},{8,11},{11,9},{9,1... | collective-permute-start | bytes 1597448 | tf_op jit(solution)/shard_map/ppermute | solution.py:111
  10.2 3.6 %collective-permute-done.3.refs_2_ = bf16[2080,128]{1,0:T(8,128)(2,1)S(1)} collective-permute-done((bf16[2080,128]{1,0:T(8,128)(2,1)S(1)}, bf16[2080,128]{1,0:T(8,128)(2,1)S(1)}, u32[]{:S(2)}, u32[]{:S(2)}) %collective-permute-start.3) | collective-permute-done | bytes 532512 | tf_op jit(solution)/shard_map/ppermute | solution.py:98
  13.9 2.1 %collective-permute-start.5 = (bf16[1040,128]{1,0:T(8,128)(2,1)S(1)}, bf16[1040,128]{1,0:T(8,128)(2,1)S(1)}, u32[]{:S(2)}, u32[]{:S(2)}) collective-permute-start(bf16[1040,128]{1,0:T(8,128)(2,1)S(1)} %slice.28), channel_id=1, source_target_pairs={{0,16},{4,12},{8,24},{12,4},{16,0},{20,28},{24,8},{28,20},{1,17},{... | collective-permute-start | bytes 798728 | tf_op jit(solution)/shard_map/ppermute | solution.py:98
  16.0 0.0 collective-permute-start.4
  16.0 4.4 %collective-permute-done.5.refs_4_ = bf16[1040,128]{1,0:T(8,128)(2,1)S(1)} collective-permute-done((bf16[1040,128]{1,0:T(8,128)(2,1)S(1)}, bf16[1040,128]{1,0:T(8,128)(2,1)S(1)}, u32[]{:S(2)}, u32[]{:S(2)}) %collective-permute-start.5) | collective-permute-done | bytes 266272 | tf_op jit(solution)/shard_map/ppermute | solution.py:98
  20.4 0.0 collective-permute-start.6
  20.4 1.2 %collective-permute-done.7.refs_0_ = bf16[2080,128]{1,0:T(8,128)(2,1)S(1)} collective-permute-done((bf16[2080,128]{1,0:T(8,128)(2,1)S(1)}, bf16[2080,128]{1,0:T(8,128)(2,1)S(1)}, u32[]{:S(2)}, u32[]{:S(2)}) %collective-permute-start.7) | collective-permute-done | bytes 532512 | tf_op jit(solution)/shard_map/ppermute | solution.py:111
  21.6 0.4 %collective-permute-done.6.refs_5_ = bf16[1040,128]{1,0:T(8,128)(2,1)S(1)} collective-permute-done((bf16[1040,128]{1,0:T(8,128)(2,1)S(1)}, bf16[1040,128]{1,0:T(8,128)(2,1)S(1)}, u32[]{:S(2)}, u32[]{:S(2)}) %collective-permute-start.6) | collective-permute-done | bytes 266272 | tf_op jit(solution)/shard_map/ppermute | solution.py:95
  21.9 0.0 collective-permute-done.4.refs_3_
  21.9 0.9 %shard_map.39 = (f32[2,128]{1,0:T(2,128)S(1)}, f32[8,128]{1,0:T(8,128)S(1)}) custom-call(bf16[2080,128]{1,0:T(8,128)(2,1)S(1)} %collective-permute-done.7.refs_0_, bf16[2080,128]{1,0:T(8,128)(2,1)S(1)} %shard_map.37.refs_0_.refs_1_, bf16[2080,128]{1,0:T(8,128)(2,1)S(1)} %collective-permute-done.3.refs_2_, ...), custom_call_target="tpu_custom_call" | custom-call | flops 536870912 | bytes 2621440 | tf_op jit(solution)/shard_map/pallas_call | solution.py:77
  22.8 2.2 %collective-permute-start.8 = (f32[4,128]{1,0:T(4,128)S(1)}, f32[4,128]{1,0:T(4,128)S(1)}, u32[]{:S(2)}, u32[]{:S(2)}) collective-permute-start(f32[4,128]{1,0:T(4,128)S(1)} %slice.23), channel_id=1, source_target_pairs={{0,16},{4,12},{8,24},{12,4},{16,0},{20,28},{24,8},{28,20},{1,17},{... | collective-permute-start | bytes 6152 | tf_op jit(solution)/shard_map/ppermute | solution.py:98
  25.0 2.5 %collective-permute-start.10 = (f32[2,128]{1,0:T(2,128)S(1)}, f32[2,128]{1,0:T(2,128)S(1)}, u32[]{:S(2)}, u32[]{:S(2)}) collective-permute-start(f32[2,128]{1,0:T(2,128)S(1)} %get-tuple-element.8), channel_id=1, source_target_pairs={{3,0},{1,3},{2,1},{0,2},{5,4},{6,7},{4,5},{7,6},{11,8},{9,11},{10,... | collective-permute-start | bytes 3080 | tf_op jit(solution)/shard_map/ppermute | solution.py:111
  27.5 0.0 collective-permute-done.8
  27.5 1.6 %collective-permute-start.9 = (f32[2,128]{1,0:T(2,128)S(1)}, f32[2,128]{1,0:T(2,128)S(1)}, u32[]{:S(2)}, u32[]{:S(2)}) collective-permute-start(f32[2,128]{1,0:T(2,128)S(1)} %slice.25), channel_id=1, source_target_pairs={{0,8},{4,20},{8,0},{12,28},{16,24},{20,4},{24,16},{28,12},{1,9},{5... | collective-permute-start | bytes 3080 | tf_op jit(solution)/shard_map/ppermute | solution.py:98
  29.1 1.3 %collective-permute-done.10 = f32[2,128]{1,0:T(2,128)S(1)} collective-permute-done((f32[2,128]{1,0:T(2,128)S(1)}, f32[2,128]{1,0:T(2,128)S(1)}, u32[]{:S(2)}, u32[]{:S(2)}) %collective-permute-start.10) | collective-permute-done | bytes 1056 | tf_op jit(solution)/shard_map/ppermute | solution.py:111
  30.4 0.8 %collective-permute-done.9 = f32[2,128]{1,0:T(2,128)S(1)} collective-permute-done((f32[2,128]{1,0:T(2,128)S(1)}, f32[2,128]{1,0:T(2,128)S(1)}, u32[]{:S(2)}, u32[]{:S(2)}) %collective-permute-start.9) | collective-permute-done | bytes 1056 | tf_op jit(solution)/shard_map/ppermute | solution.py:98
  31.2 0.1 collective-permute-start.11
  31.2 0.9 %shard_map.38 = f32[1,128]{1,0:T(1,128)S(1)} custom-call(bf16[2080,128]{1,0:T(8,128)(2,1)S(1)} %shard_map.37.refs_0_.refs_1_, bf16[2080,128]{1,0:T(8,128)(2,1)S(1)} %shard_map.37.refs_0_.refs_1_, bf16[2080,128]{1,0:T(8,128)(2,1)S(1)} %collective-permute-done.3.refs_2_, bf16[2080,128]{1,0:T(8,128)(2,1)S(1)} %collective-permute-done.4.refs_3_, ...), custom_call_target="tpu_custom_call" | custom-call | flops 268435456 | bytes 2359296 | tf_op jit(solution)/shard_map/pallas_call | solution.py:77
  32.1 0.2 collective-permute-done.11
  32.4 0.5 %bitcast_maximum_fusion = f32[128]{0:T(128)} fusion(f32[128]{0:T(128)S(1)} %collective-permute-done.11, f32[1,128]{1,0:T(1,128)S(1)} %shard_map.38, f32[2,128]{1,0:T(2,128)S(1)} %maximum_maximum_fusion), kind=kLoop, calls=%fused_computation.2 | loop fusion | flops 256 | bytes 2048 | tf_op jit(solution)/shard_map/max | solution.py:159
  (6 shorter events, 0.0 us)
Async XLA Ops:
  0.0 1.9 %collective-permute-start = (bf16[128,1024]{1,0:T(8,128)(2,1)}, bf16[128,1024]{1,0:T(8,128)(2,1)S(1)}, u32[]{:S(2)}, u32[]{:S(2)}) collective-permute-start(bf16[128,1024]{1,0:T(8,128)(2,1)} %emb_a.1), channel_id=1, source_target_pairs={{0,4},{4,0},{8,12},{12,8},{16,20},{20,16},{24,28},{28,24},{1,5},{5... | collective-permute-start | bytes 786440 | tf_op jit(solution)/shard_map/ppermute | solution.py:95
  0.5 1.4 %collective-permute-start.1 = (s32[128]{0:T(128)}, s32[128]{0:T(128)S(1)}, u32[]{:S(2)}, u32[]{:S(2)}) collective-permute-start(s32[128]{0:T(128)} %param.4), channel_id=1, source_target_pairs={{0,4},{4,0},{8,12},{12,8},{16,20},{20,16},{24,28},{28,24},{1,5},{5... | collective-permute-start | bytes 1544 | tf_op jit(solution)/shard_map/ppermute | solution.py:95
  0.5 1.4 %collective-permute-start.2 = (s32[128]{0:T(128)}, s32[128]{0:T(128)S(1)}, u32[]{:S(2)}, u32[]{:S(2)}) collective-permute-start(s32[128]{0:T(128)} %param.5), channel_id=1, source_target_pairs={{0,4},{4,0},{8,12},{12,8},{16,20},{20,16},{24,28},{28,24},{1,5},{5... | collective-permute-start | bytes 1544 | tf_op jit(solution)/shard_map/ppermute | solution.py:95
  1.9 0.7 %copy-start.1 = (s32[128]{0:T(128)S(1)}, s32[128]{0:T(128)}, u32[]{:S(2)}) copy-start(s32[128]{0:T(128)} %param.4) | copy-start | bytes 1540
  1.9 0.7 %copy-start.2 = (s32[128]{0:T(128)S(1)}, s32[128]{0:T(128)}, u32[]{:S(2)}) copy-start(s32[128]{0:T(128)} %param.5) | copy-start | bytes 1540
  2.6 0.9 %copy-start = (bf16[128,1024]{1,0:T(8,128)(2,1)S(1)}, bf16[128,1024]{1,0:T(8,128)(2,1)}, u32[]{:S(2)}) copy-start(bf16[128,1024]{1,0:T(8,128)(2,1)} %emb_a.1) | copy-start | bytes 786436
  3.7 10.1 %collective-permute-start.3 = (bf16[2080,128]{1,0:T(8,128)(2,1)S(1)}, bf16[2080,128]{1,0:T(8,128)(2,1)S(1)}, u32[]{:S(2)}, u32[]{:S(2)}) collective-permute-start(bf16[2080,128]{1,0:T(8,128)(2,1)S(1)} %shard_map.37.refs_0_.refs_1_), channel_id=1, source_target_pairs={{0,8},{4,20},{8,0},{12,28},{16,24},{20,4},{24,16},{28,12},{1,9},{5... | collective-permute-start | bytes 1597448 | tf_op jit(solution)/shard_map/ppermute | solution.py:98
  6.6 15.0 %collective-permute-start.7 = (bf16[2080,128]{1,0:T(8,128)(2,1)S(1)}, bf16[2080,128]{1,0:T(8,128)(2,1)S(1)}, u32[]{:S(2)}, u32[]{:S(2)}) collective-permute-start(bf16[2080,128]{1,0:T(8,128)(2,1)S(1)} %shard_map.37.refs_0_.refs_1_), channel_id=1, source_target_pairs={{0,3},{3,1},{1,2},{2,0},{4,5},{7,6},{5,4},{6,7},{8,11},{11,9},{9,1... | collective-permute-start | bytes 1597448 | tf_op jit(solution)/shard_map/ppermute | solution.py:111
  13.9 6.5 %collective-permute-start.5 = (bf16[1040,128]{1,0:T(8,128)(2,1)S(1)}, bf16[1040,128]{1,0:T(8,128)(2,1)S(1)}, u32[]{:S(2)}, u32[]{:S(2)}) collective-permute-start(bf16[1040,128]{1,0:T(8,128)(2,1)S(1)} %slice.28), channel_id=1, source_target_pairs={{0,16},{4,12},{8,24},{12,4},{16,0},{20,28},{24,8},{28,20},{1,17},{... | collective-permute-start | bytes 798728 | tf_op jit(solution)/shard_map/ppermute | solution.py:98
  16.0 5.9 %collective-permute-start.4 = (bf16[2080,128]{1,0:T(8,128)(2,1)S(1)}, bf16[2080,128]{1,0:T(8,128)(2,1)S(1)}, u32[]{:S(2)}, u32[]{:S(2)}) collective-permute-start(bf16[2080,128]{1,0:T(8,128)(2,1)S(1)} %collective-permute-done.3.refs_2_), channel_id=1, source_target_pairs={{0,4},{4,0},{8,12},{12,8},{16,20},{20,16},{24,28},{28,24},{1,5},{5... | collective-permute-start | bytes 1597448 | tf_op jit(solution)/shard_map/ppermute | solution.py:95
  20.4 1.5 %collective-permute-start.6 = (bf16[1040,128]{1,0:T(8,128)(2,1)S(1)}, bf16[1040,128]{1,0:T(8,128)(2,1)S(1)}, u32[]{:S(2)}, u32[]{:S(2)}) collective-permute-start(bf16[1040,128]{1,0:T(8,128)(2,1)S(1)} %collective-permute-done.5.refs_4_), channel_id=1, source_target_pairs={{0,4},{4,0},{8,12},{12,8},{16,20},{20,16},{24,28},{28,24},{1,5},{5... | collective-permute-start | bytes 798728 | tf_op jit(solution)/shard_map/ppermute | solution.py:95
  22.8 4.7 %collective-permute-start.8 = (f32[4,128]{1,0:T(4,128)S(1)}, f32[4,128]{1,0:T(4,128)S(1)}, u32[]{:S(2)}, u32[]{:S(2)}) collective-permute-start(f32[4,128]{1,0:T(4,128)S(1)} %slice.23), channel_id=1, source_target_pairs={{0,16},{4,12},{8,24},{12,4},{16,0},{20,28},{24,8},{28,20},{1,17},{... | collective-permute-start | bytes 6152 | tf_op jit(solution)/shard_map/ppermute | solution.py:98
  25.0 5.4 %collective-permute-start.10 = (f32[2,128]{1,0:T(2,128)S(1)}, f32[2,128]{1,0:T(2,128)S(1)}, u32[]{:S(2)}, u32[]{:S(2)}) collective-permute-start(f32[2,128]{1,0:T(2,128)S(1)} %get-tuple-element.8), channel_id=1, source_target_pairs={{3,0},{1,3},{2,1},{0,2},{5,4},{6,7},{4,5},{7,6},{11,8},{9,11},{10,... | collective-permute-start | bytes 3080 | tf_op jit(solution)/shard_map/ppermute | solution.py:111
  27.5 3.6 %collective-permute-start.9 = (f32[2,128]{1,0:T(2,128)S(1)}, f32[2,128]{1,0:T(2,128)S(1)}, u32[]{:S(2)}, u32[]{:S(2)}) collective-permute-start(f32[2,128]{1,0:T(2,128)S(1)} %slice.25), channel_id=1, source_target_pairs={{0,8},{4,20},{8,0},{12,28},{16,24},{20,4},{24,16},{28,12},{1,9},{5... | collective-permute-start | bytes 3080 | tf_op jit(solution)/shard_map/ppermute | solution.py:98
  31.2 1.2 %collective-permute-start.11 = (f32[128]{0:T(128)S(1)}, f32[128]{0:T(128)S(1)}, u32[]{:S(2)}, u32[]{:S(2)}) collective-permute-start(f32[128]{0:T(128)S(1)} %slice_bitcast_fusion), channel_id=1, source_target_pairs={{0,4},{4,0},{8,12},{12,8},{16,20},{20,16},{24,28},{28,24},{1,5},{5... | collective-permute-start | bytes 1544 | tf_op jit(solution)/shard_map/ppermute | solution.py:95

commit v2 on v1

v2 whole, which is shorter than its diff:
```python
import functools

import jax
import jax.numpy as jnp
from jax import lax
from jax.experimental import pallas as pl
from jax.experimental.pallas import tpu as pltpu
from jax.sharding import PartitionSpec as P

LANES = 128
META = 16


def pack_kernel(emb, clu, idx, out):
    width = emb.shape[1]
    wide = emb[...].astype(jnp.float32)
    norm = lax.rsqrt(jnp.sum(wide * wide, axis=1, keepdims=True) + 1e-06)
    unit = (wide * norm).astype(jnp.bfloat16)
    for k in range(width // LANES):
        out[pl.ds(k * LANES, LANES), :] = unit[:, k * LANES : (k + 1) * LANES]
    row = lax.broadcasted_iota(jnp.int32, (META, LANES), 0)
    index = idx[...]
    meta = jnp.where(row == 0, clu[...], jnp.where(row == 1, index >> 8, index & 255))
    out[pl.ds(width, META), :] = meta.astype(jnp.float32).astype(jnp.bfloat16)


def load_block(ref):
    width = ref.shape[0] - META
    parts = [ref[pl.ds(k * LANES, LANES), :] for k in range(width // LANES)]
    meta = ref[pl.ds(width, META), :].astype(jnp.float32)
    return jnp.concatenate(parts, axis=1), meta[0:1], meta[1:2] * 256.0 + meta[2:3]


def down(row):
    return jnp.transpose(jnp.broadcast_to(row, (LANES, LANES)))


def pair_kernel(block, mate, pair):
    step = block.shape[0]
    pair[pl.ds(0, step), :] = block[...]
    pair[pl.ds(step, step), :] = mate[...]


def join(block, mate):
    return pl.pallas_call(
        pair_kernel,
        out_shape=jax.ShapeDtypeStruct((2 * block.shape[0], LANES), block.dtype),
        in_specs=[pl.BlockSpec(memory_space=pltpu.VMEM)] * 2,
        out_specs=pl.BlockSpec(memory_space=pltpu.VMEM),
        compiler_params=pltpu.CompilerParams(vmem_limit_bytes=16 * 2**20),
    )(block, mate)


def score_kernel(queries, places, cross, *refs):
    query_ref, refs = refs[0], refs[1:]
    key_refs, outs = refs[: len(places)], refs[len(places) :]
    step = query_ref.shape[0] // queries
    loaded = [load_block(query_ref.at[pl.ds(i * step, step)]) for i in range(queries)]
    query = jnp.concatenate([block[0] for block in loaded], axis=0)
    q_clu = jnp.concatenate([down(block[1]) for block in loaded], axis=0)
    q_idx = jnp.concatenate([down(block[2]) for block in loaded], axis=0)
    row_best = jnp.full((queries * LANES, LANES), -1.0, jnp.float32)
    for first in range(0, len(places), 2):
        keys = [load_block(ref) for ref in key_refs[first : first + 2]]
        scores = lax.dot_general(
            query,
            jnp.concatenate([key[0] for key in keys], axis=0),
            (((1,), (1,)), ((), ())),
            preferred_element_type=jnp.float32,
        )
        for number, key in enumerate(keys):
            part = scores[:, number * LANES : (number + 1) * LANES]
            part = jnp.where(key[1] == q_clu, part, -1.0)
            earlier = key[2] < q_idx
            row_best = jnp.maximum(row_best, jnp.where(earlier, part, -1.0))
            if cross:
                col = jnp.max(jnp.where(earlier, -1.0, part), axis=0, keepdims=True)
                outs[1][pl.ds(places[first + number], 1), :] = col
    for i in range(queries):
        block = jnp.transpose(row_best[i * LANES : (i + 1) * LANES])
        outs[0][pl.ds(i, 1), :] = jnp.max(block, axis=0, keepdims=True)


def score(count, query, keys, places, cross):
    blocks = len(keys)
    width = keys[0].shape[0] - META
    shapes = [jax.ShapeDtypeStruct((count, LANES), jnp.float32)]
    if cross:
        shapes.append(jax.ShapeDtypeStruct((blocks, LANES), jnp.float32))
    return pl.pallas_call(
        functools.partial(score_kernel, count, places, cross),
        out_shape=shapes,
        in_specs=[pl.BlockSpec(memory_space=pltpu.VMEM)] * (1 + blocks),
        out_specs=[pl.BlockSpec(memory_space=pltpu.VMEM)] * len(shapes),
        compiler_params=pltpu.CompilerParams(vmem_limit_bytes=32 * 2**20),
        cost_estimate=pl.CostEstimate(
            flops=2 * count * blocks * LANES * LANES * width,
            bytes_accessed=2 * (count + blocks) * LANES * width,
            transcendentals=0,
        ),
    )(query, *keys)


def program(groups, blks, embedding, cluster, doc_index):
    rows, width = embedding.shape

    def swap(x):
        return lax.ppermute(x, "group", [(g, g ^ 1) for g in range(groups)])

    def turn(x, even, odd):
        return lax.ppermute(x, "group", [(g, g ^ (odd if g & 1 else even)) for g in range(groups)])

    order = [i // 2 if i % 2 == 0 else blks - 1 - i // 2 for i in range(blks)]
    rounds = max(1, blks // 4)

    def visit(x, number, back):
        pairs = []
        for g in range(groups):
            shift = number + 1 + (rounds if g & 1 else 0)
            for i in range(blks):
                a, b = order[i], order[(i + shift) % blks]
                a, b = g * blks + a, g * blks + b
                pairs.append((b, a) if back else (a, b))
        return lax.ppermute(x, ("group", "blk"), pairs)

    block = pl.pallas_call(
        pack_kernel,
        out_shape=jax.ShapeDtypeStruct((width + META, LANES), jnp.bfloat16),
        in_specs=[pl.BlockSpec(memory_space=pltpu.VMEM)] * 3,
        out_specs=pl.BlockSpec(memory_space=pltpu.VMEM),
        compiler_params=pltpu.CompilerParams(vmem_limit_bytes=16 * 2**20),
    )(embedding, cluster.reshape(1, rows), doc_index.reshape(1, rows))

    mate = swap(block)
    near = turn(block, 2, 4)
    pair = join(block, mate)
    visitors = [visit(pair, number, False) for number in range(rounds)]
    near_mate = turn(mate, 2, 4)
    far = turn(near, 4, 2)
    keys = [block, mate, near, near_mate, swap(near_mate), swap(near), far, swap(far)]
    places = [0, 1, 2, 3, 4, 5, 6, 7]
    bit = 8
    while bit < groups:
        keys = keys + [lax.ppermute(k, "group", [(g, g ^ bit) for g in range(groups)]) for k in keys]
        places = places + [p + bit for p in places]
        bit *= 2

    (own_best,) = score(1, block, keys, places, False)
    rows_back, cols = [], None
    for number, visitor in enumerate(visitors):
        row_best, col_best = score(2, visitor, keys, places, True)
        rows_back.append(row_best)
        cols = col_best if cols is None else jnp.maximum(cols, col_best)

    bit = groups // 2
    while bit > 1:
        even, odd = bit, {2: 4, 4: 2}.get(bit, bit)
        cols = jnp.maximum(cols[:bit], turn(cols[bit:], even, odd))
        bit //= 2
    chip = cols
    for number, row_best in enumerate(rows_back):
        chip = jnp.maximum(chip, visit(row_best, number, True))
    other = swap(chip[1])
    return jnp.maximum(jnp.maximum(own_best[0], chip[0]), other)


def solution(mesh):
    return jax.shard_map(
        functools.partial(program, mesh.shape["group"], mesh.shape["blk"]),
        mesh=mesh,
        in_specs=(P(("group", "blk"), None), P(("group", "blk")), P(("group", "blk"))),
        out_specs=P(("group", "blk")),
        check_vma=False,
    )
```

time: 33 us -> 30.5 us (0.924)
  waiting for transfers between devices: 12.8 us -> 10.2 us
    ppermute x4 -> x5, waiting for transfers between devices: 8.81 us -> 6.76 us  [turn(): lax.ppermute(x, 'group', [(g, g ^ (odd if g & 1 else even)) for g in rang...]
    ppermute x6 -> x5, waiting for transfers between devices: 1.52 us -> 0.22 us  [swap(): return lax.ppermute(x, 'group', [(g, g ^ 1) for g in range(groups)])]
    ppermute x2, waiting for transfers between devices: 2.48 us -> 3.24 us  [visit(): return lax.ppermute(x, ('group', 'blk'), pairs)]
    ppermute x6 -> x5, starting transfers between devices: 1.03 us -> 1.09 us  [swap(): return lax.ppermute(x, 'group', [(g, g ^ 1) for g in range(groups)])]
    ppermute x4 -> x5, starting transfers between devices: 8.7 us -> 8.64 us  [turn(): lax.ppermute(x, 'group', [(g, g ^ (odd if g & 1 else even)) for g in rang...]
    pallas_call x3 -> x4, Pallas kernels: 1.99 us -> 1.97 us  [the longest x2 1.8 us: score(): pl.pallas_call(functools.partial(score_kernel, count, places, cross), out...]
  transfers between devices with their start and end apart: 12 -> 12, of which waited for: 9 -> 5; matrix products, arithmetic and copies ran while one was open for 0% -> 0% of each run, Pallas kernels for 3% -> 3%
where the time goes in v2:
time: 30.5 us; the launch traced here: 30.4 us
  starting transfers between devices  16 us (52%)
  waiting for transfers between devices  10.2 us (33%)
  Pallas kernels  1.97 us (6%)
  local copies, waits for them, and re-layouts  1.64 us (5%)
  other arithmetic  0.52 us (2%)
    ppermute x5, starting transfers between devices, turn(): lax.ppermute(x, 'group', [(g, g ^ (odd if g & 1 else even)) for g in rang...  8.64 us
    ppermute x5, waiting for transfers between devices, turn(): lax.ppermute(x, 'group', [(g, g ^ (odd if g & 1 else even)) for g in rang...  6.76 us
    ppermute x2, starting transfers between devices, visit(): return lax.ppermute(x, ('group', 'blk'), pairs)  6.24 us
    ppermute x2, waiting for transfers between devices, visit(): return lax.ppermute(x, ('group', 'blk'), pairs)  3.24 us
    pallas_call x2, Pallas kernels, score(): pl.pallas_call(functools.partial(score_kernel, count, places, cross), out...  1.8 us
    unnamed x6, local copies, waits for them, and re-layouts  1.62 us
    ppermute x5, starting transfers between devices, swap(): return lax.ppermute(x, 'group', [(g, g ^ 1) for g in range(groups)])  1.09 us
  transfers between devices with their start and end apart: 12, of which 5 were waited for; matrix products, arithmetic and copies ran while one was open for 0% of the time, Pallas kernels for 3%

profile of v2, /device:TPU:0, one launch (start us, length us, event | category | flops | bytes accessed | tf_op | source)
XLA Modules:
  0.0 30.4 jit_solution(886977503474551026)
XLA Ops:
  0.0 0.0 copy-start.1
  0.0 0.0 copy-start.2
  0.0 0.7 %copy-done.1 = s32[128]{0:T(128)S(1)} copy-done((s32[128]{0:T(128)S(1)}, s32[128]{0:T(128)}, u32[]{:S(2)}) %copy-start.1) | copy-done | bytes 536
  0.7 0.0 copy-done.2
  0.7 0.0 copy-start
  0.7 0.9 %copy-done = bf16[128,1024]{1,0:T(8,128)(2,1)S(1)} copy-done((bf16[128,1024]{1,0:T(8,128)(2,1)S(1)}, bf16[128,1024]{1,0:T(8,128)(2,1)}, u32[]{:S(2)}) %copy-start) | copy-done | bytes 262168
  1.6 0.1 shard_map.37.refs_0_.refs_1_.block
  1.8 0.5 %collective-permute-start = (bf16[1040,128]{1,0:T(8,128)(2,1)S(1)}, bf16[1040,128]{1,0:T(8,128)(2,1)S(1)}, u32[]{:S(2)}, u32[]{:S(2)}) collective-permute-start(bf16[1040,128]{1,0:T(8,128)(2,1)S(1)} %shard_map.37.refs_0_.refs_1_.block), channel_id=1, source_target_pairs={{0,4},{4,0},{8,12},{12,8},{16,20},{20,16},{24,28},{28,24},{1,5},{5... | collective-permute-start | bytes 798728 | tf_op jit(solution)/shard_map/ppermute | solution.py:108
  2.3 2.6 %collective-permute-start.1 = (bf16[1040,128]{1,0:T(8,128)(2,1)S(1)}, bf16[1040,128]{1,0:T(8,128)(2,1)S(1)}, u32[]{:S(2)}, u32[]{:S(2)}) collective-permute-start(bf16[1040,128]{1,0:T(8,128)(2,1)S(1)} %shard_map.37.refs_0_.refs_1_.block), channel_id=1, source_target_pairs={{0,8},{4,20},{8,0},{12,28},{16,24},{20,4},{24,16},{28,12},{1,9},{5... | collective-permute-start | bytes 798728 | tf_op jit(solution)/shard_map/ppermute | solution.py:111
  4.8 0.0 collective-permute-done.refs_2_.mate
  4.9 3.7 %collective-permute-start.7 = (bf16[2080,128]{1,0:T(8,128)(2,1)S(1)}, bf16[2080,128]{1,0:T(8,128)(2,1)S(1)}, u32[]{:S(2)}, u32[]{:S(2)}) collective-permute-start(bf16[2080,128]{1,0:T(8,128)(2,1)S(1)} %shard_map.39), channel_id=1, source_target_pairs={{0,3},{3,1},{1,2},{2,0},{4,5},{7,6},{5,4},{6,7},{8,11},{11,9},{9,1... | collective-permute-start | bytes 1597448 | tf_op jit(solution)/shard_map/ppermute | solution.py:124
  8.5 1.5 %collective-permute-start.2 = (bf16[1040,128]{1,0:T(8,128)(2,1)S(1)}, bf16[1040,128]{1,0:T(8,128)(2,1)S(1)}, u32[]{:S(2)}, u32[]{:S(2)}) collective-permute-start(bf16[1040,128]{1,0:T(8,128)(2,1)S(1)} %collective-permute-done.refs_2_.mate), channel_id=1, source_target_pairs={{0,8},{4,20},{8,0},{12,28},{16,24},{20,4},{24,16},{28,12},{1,9},{5... | collective-permute-start | bytes 798728 | tf_op jit(solution)/shard_map/ppermute | solution.py:111
  10.0 0.0 collective-permute-done.1.refs_3_
  10.0 1.5 %collective-permute-start.5 = (bf16[1040,128]{1,0:T(8,128)(2,1)S(1)}, bf16[1040,128]{1,0:T(8,128)(2,1)S(1)}, u32[]{:S(2)}, u32[]{:S(2)}) collective-permute-start(bf16[1040,128]{1,0:T(8,128)(2,1)S(1)} %collective-permute-done.1.refs_3_), channel_id=1, source_target_pairs={{0,16},{4,12},{8,24},{12,4},{16,0},{20,28},{24,8},{28,20},{1,17},{... | collective-permute-start | bytes 798728 | tf_op jit(solution)/shard_map/ppermute | solution.py:111
  11.5 0.0 collective-permute-start.4
  11.5 5.9 %collective-permute-done.2.refs_4_ = bf16[1040,128]{1,0:T(8,128)(2,1)S(1)} collective-permute-done((bf16[1040,128]{1,0:T(8,128)(2,1)S(1)}, bf16[1040,128]{1,0:T(8,128)(2,1)S(1)}, u32[]{:S(2)}, u32[]{:S(2)}) %collective-permute-start.2) | collective-permute-done | bytes 266272 | tf_op jit(solution)/shard_map/ppermute | solution.py:111
  17.4 0.0 collective-permute-start.3
  17.4 0.0 collective-permute-done.5.refs_7_
  17.4 0.5 %collective-permute-start.6 = (bf16[1040,128]{1,0:T(8,128)(2,1)S(1)}, bf16[1040,128]{1,0:T(8,128)(2,1)S(1)}, u32[]{:S(2)}, u32[]{:S(2)}) collective-permute-start(bf16[1040,128]{1,0:T(8,128)(2,1)S(1)} %collective-permute-done.5.refs_7_), channel_id=1, source_target_pairs={{0,4},{4,0},{8,12},{12,8},{16,20},{20,16},{24,28},{28,24},{1,5},{5... | collective-permute-start | bytes 798728 | tf_op jit(solution)/shard_map/ppermute | solution.py:108
  17.9 0.0 collective-permute-done.4.refs_6_
  17.9 2.0 %collective-permute-done.7.refs_0_ = bf16[2080,128]{1,0:T(8,128)(2,1)S(1)} collective-permute-done((bf16[2080,128]{1,0:T(8,128)(2,1)S(1)}, bf16[2080,128]{1,0:T(8,128)(2,1)S(1)}, u32[]{:S(2)}, u32[]{:S(2)}) %collective-permute-start.7) | collective-permute-done | bytes 532512 | tf_op jit(solution)/shard_map/ppermute | solution.py:124
  19.9 0.0 collective-permute-done.3.refs_5_
  19.9 0.0 collective-permute-done.6.refs_8_
  19.9 0.9 %shard_map.40 = (f32[2,128]{1,0:T(2,128)S(1)}, f32[8,128]{1,0:T(8,128)S(1)}) custom-call(bf16[2080,128]{1,0:T(8,128)(2,1)S(1)} %collective-permute-done.7.refs_0_, bf16[1040,128]{1,0:T(8,128)(2,1)S(1)} %shard_map.37.refs_0_.refs_1_.block, bf16[1040,128]{1,0:T(8,128)(2,1)S(1)} %collective-permute-done.refs_2_.mate, ...), custom_call_target="tpu_custom_call" | custom-call | flops 536870912 | bytes 2621440 | tf_op jit(solution)/shard_map/pallas_call | solution.py:90
  20.9 1.6 %collective-permute-start.8 = (f32[4,128]{1,0:T(4,128)S(1)}, f32[4,128]{1,0:T(4,128)S(1)}, u32[]{:S(2)}, u32[]{:S(2)}) collective-permute-start(f32[4,128]{1,0:T(4,128)S(1)} %slice.19), channel_id=1, source_target_pairs={{0,16},{4,12},{8,24},{12,4},{16,0},{20,28},{24,8},{28,20},{1,17},{... | collective-permute-start | bytes 6152 | tf_op jit(solution)/shard_map/ppermute | solution.py:111
  22.4 2.6 %collective-permute-start.10 = (f32[2,128]{1,0:T(2,128)S(1)}, f32[2,128]{1,0:T(2,128)S(1)}, u32[]{:S(2)}, u32[]{:S(2)}) collective-permute-start(f32[2,128]{1,0:T(2,128)S(1)} %get-tuple-element.8), channel_id=1, source_target_pairs={{3,0},{1,3},{2,1},{0,2},{5,4},{6,7},{4,5},{7,6},{11,8},{9,11},{10,... | collective-permute-start | bytes 3080 | tf_op jit(solution)/shard_map/ppermute | solution.py:124
  25.0 0.0 collective-permute-done.8
  25.0 1.5 %collective-permute-start.9 = (f32[2,128]{1,0:T(2,128)S(1)}, f32[2,128]{1,0:T(2,128)S(1)}, u32[]{:S(2)}, u32[]{:S(2)}) collective-permute-start(f32[2,128]{1,0:T(2,128)S(1)} %slice.21), channel_id=1, source_target_pairs={{0,8},{4,20},{8,0},{12,28},{16,24},{20,4},{24,16},{28,12},{1,9},{5... | collective-permute-start | bytes 3080 | tf_op jit(solution)/shard_map/ppermute | solution.py:111
  26.6 1.2 %collective-permute-done.10 = f32[2,128]{1,0:T(2,128)S(1)} collective-permute-done((f32[2,128]{1,0:T(2,128)S(1)}, f32[2,128]{1,0:T(2,128)S(1)}, u32[]{:S(2)}, u32[]{:S(2)}) %collective-permute-start.10) | collective-permute-done | bytes 1056 | tf_op jit(solution)/shard_map/ppermute | solution.py:124
  27.8 0.9 %collective-permute-done.9 = f32[2,128]{1,0:T(2,128)S(1)} collective-permute-done((f32[2,128]{1,0:T(2,128)S(1)}, f32[2,128]{1,0:T(2,128)S(1)}, u32[]{:S(2)}, u32[]{:S(2)}) %collective-permute-start.9) | collective-permute-done | bytes 1056 | tf_op jit(solution)/shard_map/ppermute | solution.py:111
  28.7 0.1 collective-permute-start.11
  28.8 0.9 %shard_map.38 = f32[1,128]{1,0:T(1,128)S(1)} custom-call(bf16[1040,128]{1,0:T(8,128)(2,1)S(1)} %shard_map.37.refs_0_.refs_1_.block, bf16[1040,128]{1,0:T(8,128)(2,1)S(1)} %shard_map.37.refs_0_.refs_1_.block, bf16[1040,128]{1,0:T(8,128)(2,1)S(1)} %collective-permute-done.refs_2_.mate, bf16[1040,128]{1,0:T(8,128)(2,1)S(1)} %collective-permute-done.1.refs_3_, ...), custom_call_target="tpu_custom_call" | custom-call | flops 268435456 | bytes 2359296 | tf_op jit(solution)/shard_map/pallas_call | solution.py:90
  29.7 0.2 collective-permute-done.11
  29.9 0.5 %bitcast_maximum_fusion = f32[128]{0:T(128)} fusion(f32[128]{0:T(128)S(1)} %collective-permute-done.11, f32[1,128]{1,0:T(1,128)S(1)} %shard_map.38, f32[2,128]{1,0:T(2,128)S(1)} %maximum_maximum_fusion), kind=kLoop, calls=%fused_computation.2 | loop fusion | flops 256 | bytes 2048 | tf_op jit(solution)/shard_map/max | solution.py:164
  (6 shorter events, 0.1 us)
Async XLA Ops:
  0.0 0.7 %copy-start.1 = (s32[128]{0:T(128)S(1)}, s32[128]{0:T(128)}, u32[]{:S(2)}) copy-start(s32[128]{0:T(128)} %param.4) | copy-start | bytes 1540
  0.0 0.7 %copy-start.2 = (s32[128]{0:T(128)S(1)}, s32[128]{0:T(128)}, u32[]{:S(2)}) copy-start(s32[128]{0:T(128)} %param.5) | copy-start | bytes 1540
  0.7 0.9 %copy-start = (bf16[128,1024]{1,0:T(8,128)(2,1)S(1)}, bf16[128,1024]{1,0:T(8,128)(2,1)}, u32[]{:S(2)}) copy-start(bf16[128,1024]{1,0:T(8,128)(2,1)} %emb.1) | copy-start | bytes 786436
  1.8 3.1 %collective-permute-start = (bf16[1040,128]{1,0:T(8,128)(2,1)S(1)}, bf16[1040,128]{1,0:T(8,128)(2,1)S(1)}, u32[]{:S(2)}, u32[]{:S(2)}) collective-permute-start(bf16[1040,128]{1,0:T(8,128)(2,1)S(1)} %shard_map.37.refs_0_.refs_1_.block), channel_id=1, source_target_pairs={{0,4},{4,0},{8,12},{12,8},{16,20},{20,16},{24,28},{28,24},{1,5},{5... | collective-permute-start | bytes 798728 | tf_op jit(solution)/shard_map/ppermute | solution.py:108
  2.3 7.7 %collective-permute-start.1 = (bf16[1040,128]{1,0:T(8,128)(2,1)S(1)}, bf16[1040,128]{1,0:T(8,128)(2,1)S(1)}, u32[]{:S(2)}, u32[]{:S(2)}) collective-permute-start(bf16[1040,128]{1,0:T(8,128)(2,1)S(1)} %shard_map.37.refs_0_.refs_1_.block), channel_id=1, source_target_pairs={{0,8},{4,20},{8,0},{12,28},{16,24},{20,4},{24,16},{28,12},{1,9},{5... | collective-permute-start | bytes 798728 | tf_op jit(solution)/shard_map/ppermute | solution.py:111
  4.9 15.0 %collective-permute-start.7 = (bf16[2080,128]{1,0:T(8,128)(2,1)S(1)}, bf16[2080,128]{1,0:T(8,128)(2,1)S(1)}, u32[]{:S(2)}, u32[]{:S(2)}) collective-permute-start(bf16[2080,128]{1,0:T(8,128)(2,1)S(1)} %shard_map.39), channel_id=1, source_target_pairs={{0,3},{3,1},{1,2},{2,0},{4,5},{7,6},{5,4},{6,7},{8,11},{11,9},{9,1... | collective-permute-start | bytes 1597448 | tf_op jit(solution)/shard_map/ppermute | solution.py:124
  8.5 8.9 %collective-permute-start.2 = (bf16[1040,128]{1,0:T(8,128)(2,1)S(1)}, bf16[1040,128]{1,0:T(8,128)(2,1)S(1)}, u32[]{:S(2)}, u32[]{:S(2)}) collective-permute-start(bf16[1040,128]{1,0:T(8,128)(2,1)S(1)} %collective-permute-done.refs_2_.mate), channel_id=1, source_target_pairs={{0,8},{4,20},{8,0},{12,28},{16,24},{20,4},{24,16},{28,12},{1,9},{5... | collective-permute-start | bytes 798728 | tf_op jit(solution)/shard_map/ppermute | solution.py:111
  10.0 7.4 %collective-permute-start.5 = (bf16[1040,128]{1,0:T(8,128)(2,1)S(1)}, bf16[1040,128]{1,0:T(8,128)(2,1)S(1)}, u32[]{:S(2)}, u32[]{:S(2)}) collective-permute-start(bf16[1040,128]{1,0:T(8,128)(2,1)S(1)} %collective-permute-done.1.refs_3_), channel_id=1, source_target_pairs={{0,16},{4,12},{8,24},{12,4},{16,0},{20,28},{24,8},{28,20},{1,17},{... | collective-permute-start | bytes 798728 | tf_op jit(solution)/shard_map/ppermute | solution.py:111
  11.5 6.4 %collective-permute-start.4 = (bf16[1040,128]{1,0:T(8,128)(2,1)S(1)}, bf16[1040,128]{1,0:T(8,128)(2,1)S(1)}, u32[]{:S(2)}, u32[]{:S(2)}) collective-permute-start(bf16[1040,128]{1,0:T(8,128)(2,1)S(1)} %collective-permute-done.1.refs_3_), channel_id=1, source_target_pairs={{0,4},{4,0},{8,12},{12,8},{16,20},{20,16},{24,28},{28,24},{1,5},{5... | collective-permute-start | bytes 798728 | tf_op jit(solution)/shard_map/ppermute | solution.py:108
  17.4 2.5 %collective-permute-start.3 = (bf16[1040,128]{1,0:T(8,128)(2,1)S(1)}, bf16[1040,128]{1,0:T(8,128)(2,1)S(1)}, u32[]{:S(2)}, u32[]{:S(2)}) collective-permute-start(bf16[1040,128]{1,0:T(8,128)(2,1)S(1)} %collective-permute-done.2.refs_4_), channel_id=1, source_target_pairs={{0,4},{4,0},{8,12},{12,8},{16,20},{20,16},{24,28},{28,24},{1,5},{5... | collective-permute-start | bytes 798728 | tf_op jit(solution)/shard_map/ppermute | solution.py:108
  17.4 2.5 %collective-permute-start.6 = (bf16[1040,128]{1,0:T(8,128)(2,1)S(1)}, bf16[1040,128]{1,0:T(8,128)(2,1)S(1)}, u32[]{:S(2)}, u32[]{:S(2)}) collective-permute-start(bf16[1040,128]{1,0:T(8,128)(2,1)S(1)} %collective-permute-done.5.refs_7_), channel_id=1, source_target_pairs={{0,4},{4,0},{8,12},{12,8},{16,20},{20,16},{24,28},{28,24},{1,5},{5... | collective-permute-start | bytes 798728 | tf_op jit(solution)/shard_map/ppermute | solution.py:108
  20.9 4.2 %collective-permute-start.8 = (f32[4,128]{1,0:T(4,128)S(1)}, f32[4,128]{1,0:T(4,128)S(1)}, u32[]{:S(2)}, u32[]{:S(2)}) collective-permute-start(f32[4,128]{1,0:T(4,128)S(1)} %slice.19), channel_id=1, source_target_pairs={{0,16},{4,12},{8,24},{12,4},{16,0},{20,28},{24,8},{28,20},{1,17},{... | collective-permute-start | bytes 6152 | tf_op jit(solution)/shard_map/ppermute | solution.py:111
  22.4 5.4 %collective-permute-start.10 = (f32[2,128]{1,0:T(2,128)S(1)}, f32[2,128]{1,0:T(2,128)S(1)}, u32[]{:S(2)}, u32[]{:S(2)}) collective-permute-start(f32[2,128]{1,0:T(2,128)S(1)} %get-tuple-element.8), channel_id=1, source_target_pairs={{3,0},{1,3},{2,1},{0,2},{5,4},{6,7},{4,5},{7,6},{11,8},{9,11},{10,... | collective-permute-start | bytes 3080 | tf_op jit(solution)/shard_map/ppermute | solution.py:124
  25.0 3.6 %collective-permute-start.9 = (f32[2,128]{1,0:T(2,128)S(1)}, f32[2,128]{1,0:T(2,128)S(1)}, u32[]{:S(2)}, u32[]{:S(2)}) collective-permute-start(f32[2,128]{1,0:T(2,128)S(1)} %slice.21), channel_id=1, source_target_pairs={{0,8},{4,20},{8,0},{12,28},{16,24},{20,4},{24,16},{28,12},{1,9},{5... | collective-permute-start | bytes 3080 | tf_op jit(solution)/shard_map/ppermute | solution.py:111
  28.7 1.2 %collective-permute-start.11 = (f32[128]{0:T(128)S(1)}, f32[128]{0:T(128)S(1)}, u32[]{:S(2)}, u32[]{:S(2)}) collective-permute-start(f32[128]{0:T(128)S(1)} %slice_bitcast_fusion), channel_id=1, source_target_pairs={{0,4},{4,0},{8,12},{12,8},{16,20},{20,16},{24,28},{28,24},{1,5},{5... | collective-permute-start | bytes 1544 | tf_op jit(solution)/shard_map/ppermute | solution.py:108

commit v3 on v2

--- a/solution.py
+++ b/solution.py
@@ -11,8 +11,16 @@
 META = 16
 
 
-def pack_kernel(emb, clu, idx, out):
+def pack_kernel(emb_hbm, clu_hbm, idx_hbm, out, emb, clu, idx, sems):
     width = emb.shape[1]
+    copies = [
+        pltpu.make_async_copy(source, target, sems.at[i])
+        for i, (source, target) in enumerate(((emb_hbm, emb), (clu_hbm, clu), (idx_hbm, idx)))
+    ]
+    for copy in copies:
+        copy.start()
+    for copy in copies:
+        copy.wait()
     wide = emb[...].astype(jnp.float32)
     norm = lax.rsqrt(jnp.sum(wide * wide, axis=1, keepdims=True) + 1e-06)
     unit = (wide * norm).astype(jnp.bfloat16)
@@ -101,6 +109,22 @@
     )(query, *keys)
 
 
+def merge_kernel(fold, col, col_other, row_other, own, odd, near, mix, chip):
+    def both(p):
+        q = (p & ~6 | (p & 2) << 1 | (p & 4) >> 1) ^ 1
+        return jnp.maximum(col[pl.ds(p, 1), :], col_other[pl.ds(q, 1), :])
+
+    for i in range(2):
+        near[pl.ds(i, 1), :] = both(2 + i)
+        if fold:
+            row = row_other[pl.ds(1 - i, 1), :]
+            mix[pl.ds(i, 1), :] = jnp.where(odd[0] == 1, row, both(6 + i))
+        else:
+            mix[pl.ds(i, 1), :] = both(6 + i)
+    chip[pl.ds(0, 1), :] = jnp.maximum(own[...], both(0))
+    chip[pl.ds(1, 1), :] = both(1)
+
+
 def program(groups, blks, embedding, cluster, doc_index):
     rows, width = embedding.shape
 
@@ -126,8 +150,14 @@
     block = pl.pallas_call(
         pack_kernel,
         out_shape=jax.ShapeDtypeStruct((width + META, LANES), jnp.bfloat16),
-        in_specs=[pl.BlockSpec(memory_space=pltpu.VMEM)] * 3,
+        in_specs=[pl.BlockSpec(memory_space=pltpu.HBM)] * 3,
         out_specs=pl.BlockSpec(memory_space=pltpu.VMEM),
+        scratch_shapes=[
+            pltpu.VMEM((rows, width), embedding.dtype),
+            pltpu.VMEM((1, rows), jnp.int32),
+            pltpu.VMEM((1, rows), jnp.int32),
+            pltpu.SemaphoreType.DMA((3,)),
+        ],
         compiler_params=pltpu.CompilerParams(vmem_limit_bytes=16 * 2**20),
     )(embedding, cluster.reshape(1, rows), doc_index.reshape(1, rows))
 
@@ -153,15 +183,34 @@
         cols = col_best if cols is None else jnp.maximum(cols, col_best)
 
     bit = groups // 2
-    while bit > 1:
-        even, odd = bit, {2: 4, 4: 2}.get(bit, bit)
-        cols = jnp.maximum(cols[:bit], turn(cols[bit:], even, odd))
+    while bit > 4:
+        cols = jnp.maximum(cols[:bit], turn(cols[bit:], bit, bit))
         bit //= 2
-    chip = cols
-    for number, row_best in enumerate(rows_back):
-        chip = jnp.maximum(chip, visit(row_best, number, True))
-    other = swap(chip[1])
-    return jnp.maximum(jnp.maximum(own_best[0], chip[0]), other)
+
+    fold = rounds == 1
+    odd = (lax.axis_index("group") & 1).astype(jnp.int32).reshape(1)
+    small = jax.ShapeDtypeStruct((2, LANES), jnp.float32)
+    near_out, mix_out, chip = pl.pallas_call(
+        functools.partial(merge_kernel, fold),
+        out_shape=[small] * 3,
+        in_specs=[pl.BlockSpec(memory_space=pltpu.VMEM)] * 4
+        + [pl.BlockSpec(memory_space=pltpu.SMEM)],
+        out_specs=[pl.BlockSpec(memory_space=pltpu.VMEM)] * 3,
+        compiler_params=pltpu.CompilerParams(vmem_limit_bytes=4 * 2**20),
+    )(cols, swap(cols), swap(rows_back[0]), own_best, odd)
+    chip = jnp.maximum(chip, turn(near_out, 2, 4))
+    pairs = []
+    for g in range(groups):
+        for i in range(blks):
+            if fold and g & 1:
+                pairs.append((g * blks + order[(i + 1) % blks], g * blks + order[i]))
+            else:
+                pairs.append((g * blks + i, (g ^ 6) * blks + i))
+    chip = jnp.maximum(chip, lax.ppermute(mix_out, ("group", "blk"), pairs))
+    if not fold:
+        for number, row_best in enumerate(rows_back):
+            chip = jnp.maximum(chip, visit(row_best, number, True))
+    return jnp.maximum(chip[0], swap(chip[1]))
 
 
 def solution(mesh):

time: 30.5 us -> 30.3 us (level)
  starting transfers between devices: 16 us -> 13.9 us
  waiting for transfers between devices: 10.2 us -> 12 us
    ppermute x2 -> x1, starting transfers between devices: 6.24 us -> 3.65 us  [visit(): return lax.ppermute(x, ('group', 'blk'), pairs)]
    ppermute x5 -> x4, starting transfers between devices: 8.64 us -> 6.11 us  [turn(): lax.ppermute(x, 'group', [(g, g ^ (odd if g & 1 else even)) for g in rang...]
    ppermute x0 -> x1, starting transfers between devices: none -> 2.45 us  [program(): chip = jnp.maximum(chip, lax.ppermute(mix_out, ('group', 'blk'), pairs))]
    ppermute x0 -> x1, waiting for transfers between devices: none -> 1.5 us  [program(): chip = jnp.maximum(chip, lax.ppermute(mix_out, ('group', 'blk'), pairs))]
    ppermute x2 -> x1, waiting for transfers between devices: 3.24 us -> 1.99 us  [visit(): return lax.ppermute(x, ('group', 'blk'), pairs)]
    ppermute x5 -> x7, waiting for transfers between devices: 0.22 us -> 1.12 us  [swap(): return lax.ppermute(x, 'group', [(g, g ^ 1) for g in range(groups)])]
    ppermute x5 -> x4, waiting for transfers between devices: 6.76 us -> 7.4 us  [turn(): lax.ppermute(x, 'group', [(g, g ^ (odd if g & 1 else even)) for g in rang...]
    ppermute x5 -> x7, starting transfers between devices: 1.09 us -> 1.66 us  [swap(): return lax.ppermute(x, 'group', [(g, g ^ 1) for g in range(groups)])]
  transfers between devices with their start and end apart: 12 -> 13, of which waited for: 5 -> 5; matrix products, arithmetic and copies ran while one was open for 0% -> 0% of each run, Pallas kernels for 3% -> 3%
where the time goes in v3:
time: 30.3 us; the launch traced here: 30.2 us
  starting transfers between devices  13.9 us (46%)
  waiting for transfers between devices  12 us (40%)
  Pallas kernels  2.05 us (7%)
  local copies, waits for them, and re-layouts  1.63 us (5%)
  other arithmetic  0.52 us (2%)
    ppermute x4, waiting for transfers between devices, turn(): lax.ppermute(x, 'group', [(g, g ^ (odd if g & 1 else even)) for g in rang...  7.4 us
    ppermute x4, starting transfers between devices, turn(): lax.ppermute(x, 'group', [(g, g ^ (odd if g & 1 else even)) for g in rang...  6.11 us
    ppermute x1, starting transfers between devices, visit(): return lax.ppermute(x, ('group', 'blk'), pairs)  3.65 us
    ppermute x1, starting transfers between devices, program(): chip = jnp.maximum(chip, lax.ppermute(mix_out, ('group', 'blk'), pairs))  2.45 us
    ppermute x1, waiting for transfers between devices, visit(): return lax.ppermute(x, ('group', 'blk'), pairs)  1.99 us
    pallas_call x2, Pallas kernels, score(): pl.pallas_call(functools.partial(score_kernel, count, places, cross), out...  1.81 us
    ppermute x7, starting transfers between devices, swap(): return lax.ppermute(x, 'group', [(g, g ^ 1) for g in range(groups)])  1.66 us
    unnamed x6, local copies, waits for them, and re-layouts  1.62 us
  transfers between devices with their start and end apart: 13, of which 5 were waited for; matrix products, arithmetic and copies ran while one was open for 0% of the time, Pallas kernels for 3%

profile of v3, /device:TPU:0, one launch (start us, length us, event | category | flops | bytes accessed | tf_op | source)
XLA Modules:
  0.0 30.2 jit_solution(13078300094624411461)
XLA Ops:
  0.0 0.0 copy-start.1
  0.0 0.0 copy-start.2
  0.0 0.7 %copy-done.1 = s32[128]{0:T(128)S(1)} copy-done((s32[128]{0:T(128)S(1)}, s32[128]{0:T(128)}, u32[]{:S(2)}) %copy-start.1) | copy-done | bytes 536
  0.7 0.0 copy-done.2
  0.7 0.0 copy-start
  0.7 0.9 %copy-done = bf16[128,1024]{1,0:T(8,128)(2,1)S(1)} copy-done((bf16[128,1024]{1,0:T(8,128)(2,1)S(1)}, bf16[128,1024]{1,0:T(8,128)(2,1)}, u32[]{:S(2)}) %copy-start) | copy-done | bytes 262168
  1.6 0.2 shard_map.37.block.refs_1_.refs_0_
  1.8 0.5 %collective-permute-start = (bf16[1040,128]{1,0:T(8,128)(2,1)S(1)}, bf16[1040,128]{1,0:T(8,128)(2,1)S(1)}, u32[]{:S(2)}, u32[]{:S(2)}) collective-permute-start(bf16[1040,128]{1,0:T(8,128)(2,1)S(1)} %shard_map.37.block.refs_1_.refs_0_), channel_id=1, source_target_pairs={{0,4},{4,0},{8,12},{12,8},{16,20},{20,16},{24,28},{28,24},{1,5},{5... | collective-permute-start | bytes 798728 | tf_op jit(solution)/shard_map/ppermute | solution.py:132
  2.3 2.6 %collective-permute-start.2 = (bf16[1040,128]{1,0:T(8,128)(2,1)S(1)}, bf16[1040,128]{1,0:T(8,128)(2,1)S(1)}, u32[]{:S(2)}, u32[]{:S(2)}) collective-permute-start(bf16[1040,128]{1,0:T(8,128)(2,1)S(1)} %shard_map.37.block.refs_1_.refs_0_), channel_id=1, source_target_pairs={{0,8},{4,20},{8,0},{12,28},{16,24},{20,4},{24,16},{28,12},{1,9},{5... | collective-permute-start | bytes 798728 | tf_op jit(solution)/shard_map/ppermute | solution.py:135
  4.9 0.0 collective-permute-done.mate.refs_2_
  4.9 3.7 %collective-permute-start.1 = (bf16[2080,128]{1,0:T(8,128)(2,1)S(1)}, bf16[2080,128]{1,0:T(8,128)(2,1)S(1)}, u32[]{:S(2)}, u32[]{:S(2)}) collective-permute-start(bf16[2080,128]{1,0:T(8,128)(2,1)S(1)} %shard_map.38), channel_id=1, source_target_pairs={{0,3},{3,1},{1,2},{2,0},{4,5},{7,6},{5,4},{6,7},{8,11},{11,9},{9,1... | collective-permute-start | bytes 1597448 | tf_op jit(solution)/shard_map/ppermute | solution.py:148
  8.6 1.5 %collective-permute-start.3 = (bf16[1040,128]{1,0:T(8,128)(2,1)S(1)}, bf16[1040,128]{1,0:T(8,128)(2,1)S(1)}, u32[]{:S(2)}, u32[]{:S(2)}) collective-permute-start(bf16[1040,128]{1,0:T(8,128)(2,1)S(1)} %collective-permute-done.mate.refs_2_), channel_id=1, source_target_pairs={{0,8},{4,20},{8,0},{12,28},{16,24},{20,4},{24,16},{28,12},{1,9},{5... | collective-permute-start | bytes 798728 | tf_op jit(solution)/shard_map/ppermute | solution.py:135
  10.1 0.0 collective-permute-done.2.refs_3_
  10.1 1.5 %collective-permute-start.6 = (bf16[1040,128]{1,0:T(8,128)(2,1)S(1)}, bf16[1040,128]{1,0:T(8,128)(2,1)S(1)}, u32[]{:S(2)}, u32[]{:S(2)}) collective-permute-start(bf16[1040,128]{1,0:T(8,128)(2,1)S(1)} %collective-permute-done.2.refs_3_), channel_id=1, source_target_pairs={{0,16},{4,12},{8,24},{12,4},{16,0},{20,28},{24,8},{28,20},{1,17},{... | collective-permute-start | bytes 798728 | tf_op jit(solution)/shard_map/ppermute | solution.py:135
  11.6 0.0 collective-permute-start.5
  11.6 5.9 %collective-permute-done.3.refs_4_ = bf16[1040,128]{1,0:T(8,128)(2,1)S(1)} collective-permute-done((bf16[1040,128]{1,0:T(8,128)(2,1)S(1)}, bf16[1040,128]{1,0:T(8,128)(2,1)S(1)}, u32[]{:S(2)}, u32[]{:S(2)}) %collective-permute-start.3) | collective-permute-done | bytes 266272 | tf_op jit(solution)/shard_map/ppermute | solution.py:135
  17.5 0.0 collective-permute-start.4
  17.5 0.0 collective-permute-done.6.refs_7_
  17.5 0.5 %collective-permute-start.7 = (bf16[1040,128]{1,0:T(8,128)(2,1)S(1)}, bf16[1040,128]{1,0:T(8,128)(2,1)S(1)}, u32[]{:S(2)}, u32[]{:S(2)}) collective-permute-start(bf16[1040,128]{1,0:T(8,128)(2,1)S(1)} %collective-permute-done.6.refs_7_), channel_id=1, source_target_pairs={{0,4},{4,0},{8,12},{12,8},{16,20},{20,16},{24,28},{28,24},{1,5},{5... | collective-permute-start | bytes 798728 | tf_op jit(solution)/shard_map/ppermute | solution.py:132
  18.0 0.0 collective-permute-done.5.refs_6_
  18.0 2.0 %collective-permute-done.1.refs_0_ = bf16[2080,128]{1,0:T(8,128)(2,1)S(1)} collective-permute-done((bf16[2080,128]{1,0:T(8,128)(2,1)S(1)}, bf16[2080,128]{1,0:T(8,128)(2,1)S(1)}, u32[]{:S(2)}, u32[]{:S(2)}) %collective-permute-start.1) | collective-permute-done | bytes 532512 | tf_op jit(solution)/shard_map/ppermute | solution.py:148
  20.0 0.0 collective-permute-done.4.refs_5_
  20.0 0.0 collective-permute-done.7.refs_8_
  20.0 0.9 %shard_map.39 = (f32[2,128]{1,0:T(2,128)S(1)}, f32[8,128]{1,0:T(8,128)S(1)}) custom-call(bf16[2080,128]{1,0:T(8,128)(2,1)S(1)} %collective-permute-done.1.refs_0_, bf16[1040,128]{1,0:T(8,128)(2,1)S(1)} %shard_map.37.block.refs_1_.refs_0_, bf16[1040,128]{1,0:T(8,128)(2,1)S(1)} %collective-permute-done.mate.refs_2_, ...), custom_call_target="tpu_custom_call" | custom-call | flops 536870912 | bytes 2621440 | tf_op jit(solution)/shard_map/pallas_call | solution.py:98
  20.9 0.1 collective-permute-start.8
  21.0 0.5 %collective-permute-start.9 = (f32[2,128]{1,0:T(2,128)S(1)}, f32[2,128]{1,0:T(2,128)S(1)}, u32[]{:S(2)}, u32[]{:S(2)}) collective-permute-start(f32[2,128]{1,0:T(2,128)S(1)} %get-tuple-element.11), channel_id=1, source_target_pairs={{0,4},{4,0},{8,12},{12,8},{16,20},{20,16},{24,28},{28,24},{1,5},{5... | collective-permute-start | bytes 3080 | tf_op jit(solution)/shard_map/ppermute | solution.py:132
  21.5 0.9 %shard_map.40.own = f32[1,128]{1,0:T(1,128)S(1)} custom-call(bf16[1040,128]{1,0:T(8,128)(2,1)S(1)} %shard_map.37.block.refs_1_.refs_0_, bf16[1040,128]{1,0:T(8,128)(2,1)S(1)} %shard_map.37.block.refs_1_.refs_0_, bf16[1040,128]{1,0:T(8,128)(2,1)S(1)} %collective-permute-done.mate.refs_2_, bf16[1040,128]{1,0:T(8,128)(2,1)S(1)} %collective-permute-done.2.refs_3_, ...), custom_call_target="tpu_custom_call" | custom-call | flops 268435456 | bytes 2359296 | tf_op jit(solution)/shard_map/pallas_call | solution.py:98
  22.4 0.0 collective-permute-done.9.row_other
  22.4 0.0 collective-permute-done.8.col_other
  22.4 2.5 %collective-permute-start.11 = (f32[2,128]{1,0:T(2,128)S(1)}, f32[2,128]{1,0:T(2,128)S(1)}, u32[]{:S(2)}, u32[]{:S(2)}) collective-permute-start(f32[2,128]{1,0:T(2,128)S(1)} %get-tuple-element.14), channel_id=1, source_target_pairs={{0,24},{1,25},{2,26},{3,27},{7,4},{5,7},{6,5},{4,6},{8,16},{9,17},... | collective-permute-start | bytes 3080 | tf_op jit(solution)/shard_map/ppermute | solution.py:209
  24.9 0.6 %collective-permute-start.10 = (f32[2,128]{1,0:T(2,128)S(1)}, f32[2,128]{1,0:T(2,128)S(1)}, u32[]{:S(2)}, u32[]{:S(2)}) collective-permute-start(f32[2,128]{1,0:T(2,128)S(1)} %get-tuple-element.13), channel_id=1, source_target_pairs={{0,8},{4,20},{8,0},{12,28},{16,24},{20,4},{24,16},{28,12},{1,9},{5... | collective-permute-start | bytes 3080 | tf_op jit(solution)/shard_map/ppermute | solution.py:135
  25.5 1.5 %collective-permute-done.11 = f32[2,128]{1,0:T(2,128)S(1)} collective-permute-done((f32[2,128]{1,0:T(2,128)S(1)}, f32[2,128]{1,0:T(2,128)S(1)}, u32[]{:S(2)}, u32[]{:S(2)}) %collective-permute-start.11) | collective-permute-done | bytes 1056 | tf_op jit(solution)/shard_map/ppermute | solution.py:209
  27.0 1.5 %collective-permute-done.10 = f32[2,128]{1,0:T(2,128)S(1)} collective-permute-done((f32[2,128]{1,0:T(2,128)S(1)}, f32[2,128]{1,0:T(2,128)S(1)}, u32[]{:S(2)}, u32[]{:S(2)}) %collective-permute-start.10) | collective-permute-done | bytes 1056 | tf_op jit(solution)/shard_map/ppermute | solution.py:135
  28.5 0.1 collective-permute-start.12
  28.5 1.1 %collective-permute-done.12 = f32[128]{0:T(128)S(1)} collective-permute-done((f32[128]{0:T(128)S(1)}, f32[128]{0:T(128)S(1)}, u32[]{:S(2)}, u32[]{:S(2)}) %collective-permute-start.12) | collective-permute-done | bytes 544 | tf_op jit(solution)/shard_map/ppermute | solution.py:132
  29.7 0.5 %bitcast_maximum_fusion = f32[128]{0:T(128)} fusion(f32[128]{0:T(128)S(1)} %collective-permute-done.12, f32[2,128]{1,0:T(2,128)S(1)} %maximum_maximum_fusion), kind=kLoop, calls=%fused_computation.1 | loop fusion | flops 128 | bytes 1536 | tf_op jit(solution)/shard_map/max | solution.py:213
  (4 shorter events, 0.1 us)
Async XLA Ops:
  0.0 0.7 %copy-start.1 = (s32[128]{0:T(128)S(1)}, s32[128]{0:T(128)}, u32[]{:S(2)}) copy-start(s32[128]{0:T(128)} %param.4) | copy-start | bytes 1540
  0.0 0.7 %copy-start.2 = (s32[128]{0:T(128)S(1)}, s32[128]{0:T(128)}, u32[]{:S(2)}) copy-start(s32[128]{0:T(128)} %param.5) | copy-start | bytes 1540
  0.7 0.9 %copy-start = (bf16[128,1024]{1,0:T(8,128)(2,1)S(1)}, bf16[128,1024]{1,0:T(8,128)(2,1)}, u32[]{:S(2)}) copy-start(bf16[128,1024]{1,0:T(8,128)(2,1)} %emb_hbm.1) | copy-start | bytes 786436
  1.8 3.1 %collective-permute-start = (bf16[1040,128]{1,0:T(8,128)(2,1)S(1)}, bf16[1040,128]{1,0:T(8,128)(2,1)S(1)}, u32[]{:S(2)}, u32[]{:S(2)}) collective-permute-start(bf16[1040,128]{1,0:T(8,128)(2,1)S(1)} %shard_map.37.block.refs_1_.refs_0_), channel_id=1, source_target_pairs={{0,4},{4,0},{8,12},{12,8},{16,20},{20,16},{24,28},{28,24},{1,5},{5... | collective-permute-start | bytes 798728 | tf_op jit(solution)/shard_map/ppermute | solution.py:132
  2.3 7.7 %collective-permute-start.2 = (bf16[1040,128]{1,0:T(8,128)(2,1)S(1)}, bf16[1040,128]{1,0:T(8,128)(2,1)S(1)}, u32[]{:S(2)}, u32[]{:S(2)}) collective-permute-start(bf16[1040,128]{1,0:T(8,128)(2,1)S(1)} %shard_map.37.block.refs_1_.refs_0_), channel_id=1, source_target_pairs={{0,8},{4,20},{8,0},{12,28},{16,24},{20,4},{24,16},{28,12},{1,9},{5... | collective-permute-start | bytes 798728 | tf_op jit(solution)/shard_map/ppermute | solution.py:135
  4.9 15.0 %collective-permute-start.1 = (bf16[2080,128]{1,0:T(8,128)(2,1)S(1)}, bf16[2080,128]{1,0:T(8,128)(2,1)S(1)}, u32[]{:S(2)}, u32[]{:S(2)}) collective-permute-start(bf16[2080,128]{1,0:T(8,128)(2,1)S(1)} %shard_map.38), channel_id=1, source_target_pairs={{0,3},{3,1},{1,2},{2,0},{4,5},{7,6},{5,4},{6,7},{8,11},{11,9},{9,1... | collective-permute-start | bytes 1597448 | tf_op jit(solution)/shard_map/ppermute | solution.py:148
  8.6 8.9 %collective-permute-start.3 = (bf16[1040,128]{1,0:T(8,128)(2,1)S(1)}, bf16[1040,128]{1,0:T(8,128)(2,1)S(1)}, u32[]{:S(2)}, u32[]{:S(2)}) collective-permute-start(bf16[1040,128]{1,0:T(8,128)(2,1)S(1)} %collective-permute-done.mate.refs_2_), channel_id=1, source_target_pairs={{0,8},{4,20},{8,0},{12,28},{16,24},{20,4},{24,16},{28,12},{1,9},{5... | collective-permute-start | bytes 798728 | tf_op jit(solution)/shard_map/ppermute | solution.py:135
  10.1 7.4 %collective-permute-start.6 = (bf16[1040,128]{1,0:T(8,128)(2,1)S(1)}, bf16[1040,128]{1,0:T(8,128)(2,1)S(1)}, u32[]{:S(2)}, u32[]{:S(2)}) collective-permute-start(bf16[1040,128]{1,0:T(8,128)(2,1)S(1)} %collective-permute-done.2.refs_3_), channel_id=1, source_target_pairs={{0,16},{4,12},{8,24},{12,4},{16,0},{20,28},{24,8},{28,20},{1,17},{... | collective-permute-start | bytes 798728 | tf_op jit(solution)/shard_map/ppermute | solution.py:135
  11.6 6.4 %collective-permute-start.5 = (bf16[1040,128]{1,0:T(8,128)(2,1)S(1)}, bf16[1040,128]{1,0:T(8,128)(2,1)S(1)}, u32[]{:S(2)}, u32[]{:S(2)}) collective-permute-start(bf16[1040,128]{1,0:T(8,128)(2,1)S(1)} %collective-permute-done.2.refs_3_), channel_id=1, source_target_pairs={{0,4},{4,0},{8,12},{12,8},{16,20},{20,16},{24,28},{28,24},{1,5},{5... | collective-permute-start | bytes 798728 | tf_op jit(solution)/shard_map/ppermute | solution.py:132
  17.5 2.5 %collective-permute-start.4 = (bf16[1040,128]{1,0:T(8,128)(2,1)S(1)}, bf16[1040,128]{1,0:T(8,128)(2,1)S(1)}, u32[]{:S(2)}, u32[]{:S(2)}) collective-permute-start(bf16[1040,128]{1,0:T(8,128)(2,1)S(1)} %collective-permute-done.3.refs_4_), channel_id=1, source_target_pairs={{0,4},{4,0},{8,12},{12,8},{16,20},{20,16},{24,28},{28,24},{1,5},{5... | collective-permute-start | bytes 798728 | tf_op jit(solution)/shard_map/ppermute | solution.py:132
  17.5 2.5 %collective-permute-start.7 = (bf16[1040,128]{1,0:T(8,128)(2,1)S(1)}, bf16[1040,128]{1,0:T(8,128)(2,1)S(1)}, u32[]{:S(2)}, u32[]{:S(2)}) collective-permute-start(bf16[1040,128]{1,0:T(8,128)(2,1)S(1)} %collective-permute-done.6.refs_7_), channel_id=1, source_target_pairs={{0,4},{4,0},{8,12},{12,8},{16,20},{20,16},{24,28},{28,24},{1,5},{5... | collective-permute-start | bytes 798728 | tf_op jit(solution)/shard_map/ppermute | solution.py:132
  20.9 1.5 %collective-permute-start.8 = (f32[8,128]{1,0:T(8,128)S(1)}, f32[8,128]{1,0:T(8,128)S(1)}, u32[]{:S(2)}, u32[]{:S(2)}) collective-permute-start(f32[8,128]{1,0:T(8,128)S(1)} %get-tuple-element.10.col), channel_id=1, source_target_pairs={{0,4},{4,0},{8,12},{12,8},{16,20},{20,16},{24,28},{28,24},{1,5},{5... | collective-permute-start | bytes 12296 | tf_op jit(solution)/shard_map/ppermute | solution.py:132
  21.0 1.4 %collective-permute-start.9 = (f32[2,128]{1,0:T(2,128)S(1)}, f32[2,128]{1,0:T(2,128)S(1)}, u32[]{:S(2)}, u32[]{:S(2)}) collective-permute-start(f32[2,128]{1,0:T(2,128)S(1)} %get-tuple-element.11), channel_id=1, source_target_pairs={{0,4},{4,0},{8,12},{12,8},{16,20},{20,16},{24,28},{28,24},{1,5},{5... | collective-permute-start | bytes 3080 | tf_op jit(solution)/shard_map/ppermute | solution.py:132
  22.4 4.5 %collective-permute-start.11 = (f32[2,128]{1,0:T(2,128)S(1)}, f32[2,128]{1,0:T(2,128)S(1)}, u32[]{:S(2)}, u32[]{:S(2)}) collective-permute-start(f32[2,128]{1,0:T(2,128)S(1)} %get-tuple-element.14), channel_id=1, source_target_pairs={{0,24},{1,25},{2,26},{3,27},{7,4},{5,7},{6,5},{4,6},{8,16},{9,17},... | collective-permute-start | bytes 3080 | tf_op jit(solution)/shard_map/ppermute | solution.py:209
  24.9 3.6 %collective-permute-start.10 = (f32[2,128]{1,0:T(2,128)S(1)}, f32[2,128]{1,0:T(2,128)S(1)}, u32[]{:S(2)}, u32[]{:S(2)}) collective-permute-start(f32[2,128]{1,0:T(2,128)S(1)} %get-tuple-element.13), channel_id=1, source_target_pairs={{0,8},{4,20},{8,0},{12,28},{16,24},{20,4},{24,16},{28,12},{1,9},{5... | collective-permute-start | bytes 3080 | tf_op jit(solution)/shard_map/ppermute | solution.py:135
  28.5 1.2 %collective-permute-start.12 = (f32[128]{0:T(128)S(1)}, f32[128]{0:T(128)S(1)}, u32[]{:S(2)}, u32[]{:S(2)}) collective-permute-start(f32[128]{0:T(128)S(1)} %slice_bitcast_fusion), channel_id=1, source_target_pairs={{0,4},{4,0},{8,12},{12,8},{16,20},{20,16},{24,28},{28,24},{1,5},{5... | collective-permute-start | bytes 1544 | tf_op jit(solution)/shard_map/ppermute | solution.py:132

commit v4 on v3

--- a/solution.py
+++ b/solution.py
@@ -11,25 +11,21 @@
 META = 16
 
 
-def pack_kernel(emb_hbm, clu_hbm, idx_hbm, out, emb, clu, idx, sems):
+def meta_kernel(clu, idx, out):
+    row = lax.broadcasted_iota(jnp.int32, (META, LANES), 0)
+    index = idx[...]
+    meta = jnp.where(row == 0, clu[...], jnp.where(row == 1, index >> 8, index & 255))
+    out[...] = meta.astype(jnp.float32).astype(jnp.bfloat16)
+
+
+def pack_kernel(emb, meta, out):
     width = emb.shape[1]
-    copies = [
-        pltpu.make_async_copy(source, target, sems.at[i])
-        for i, (source, target) in enumerate(((emb_hbm, emb), (clu_hbm, clu), (idx_hbm, idx)))
-    ]
-    for copy in copies:
-        copy.start()
-    for copy in copies:
-        copy.wait()
     wide = emb[...].astype(jnp.float32)
     norm = lax.rsqrt(jnp.sum(wide * wide, axis=1, keepdims=True) + 1e-06)
     unit = (wide * norm).astype(jnp.bfloat16)
     for k in range(width // LANES):
         out[pl.ds(k * LANES, LANES), :] = unit[:, k * LANES : (k + 1) * LANES]
-    row = lax.broadcasted_iota(jnp.int32, (META, LANES), 0)
-    index = idx[...]
-    meta = jnp.where(row == 0, clu[...], jnp.where(row == 1, index >> 8, index & 255))
-    out[pl.ds(width, META), :] = meta.astype(jnp.float32).astype(jnp.bfloat16)
+    out[pl.ds(width, META), :] = meta[...]
 
 
 def load_block(ref):
@@ -61,7 +57,8 @@
 
 def score_kernel(queries, places, cross, *refs):
     query_ref, refs = refs[0], refs[1:]
-    key_refs, outs = refs[: len(places)], refs[len(places) :]
+    key_refs, out = refs[:-1], refs[-1]
+    base = len(places) if cross else 0
     step = query_ref.shape[0] // queries
     loaded = [load_block(query_ref.at[pl.ds(i * step, step)]) for i in range(queries)]
     query = jnp.concatenate([block[0] for block in loaded], axis=0)
@@ -83,23 +80,20 @@
             row_best = jnp.maximum(row_best, jnp.where(earlier, part, -1.0))
             if cross:
                 col = jnp.max(jnp.where(earlier, -1.0, part), axis=0, keepdims=True)
-                outs[1][pl.ds(places[first + number], 1), :] = col
+                out[pl.ds(places[first + number], 1), :] = col
     for i in range(queries):
         block = jnp.transpose(row_best[i * LANES : (i + 1) * LANES])
-        outs[0][pl.ds(i, 1), :] = jnp.max(block, axis=0, keepdims=True)
+        out[pl.ds(base + i, 1), :] = jnp.max(block, axis=0, keepdims=True)
 
 
 def score(count, query, keys, places, cross):
     blocks = len(keys)
     width = keys[0].shape[0] - META
-    shapes = [jax.ShapeDtypeStruct((count, LANES), jnp.float32)]
-    if cross:
-        shapes.append(jax.ShapeDtypeStruct((blocks, LANES), jnp.float32))
     return pl.pallas_call(
         functools.partial(score_kernel, count, places, cross),
-        out_shape=shapes,
+        out_shape=jax.ShapeDtypeStruct((count + blocks * cross, LANES), jnp.float32),
         in_specs=[pl.BlockSpec(memory_space=pltpu.VMEM)] * (1 + blocks),
-        out_specs=[pl.BlockSpec(memory_space=pltpu.VMEM)] * len(shapes),
+        out_specs=pl.BlockSpec(memory_space=pltpu.VMEM),
         compiler_params=pltpu.CompilerParams(vmem_limit_bytes=32 * 2**20),
         cost_estimate=pl.CostEstimate(
             flops=2 * count * blocks * LANES * LANES * width,
@@ -109,18 +103,22 @@
     )(query, *keys)
 
 
-def merge_kernel(fold, col, col_other, row_other, own, odd, near, mix, chip):
+def merge_kernel(fold, res, other, own, near, mix, chip):
     def both(p):
         q = (p & ~6 | (p & 2) << 1 | (p & 4) >> 1) ^ 1
-        return jnp.maximum(col[pl.ds(p, 1), :], col_other[pl.ds(q, 1), :])
+        return jnp.maximum(res[pl.ds(p, 1), :], other[pl.ds(q, 1), :])
 
     for i in range(2):
         near[pl.ds(i, 1), :] = both(2 + i)
-        if fold:
-            row = row_other[pl.ds(1 - i, 1), :]
-            mix[pl.ds(i, 1), :] = jnp.where(odd[0] == 1, row, both(6 + i))
-        else:
-            mix[pl.ds(i, 1), :] = both(6 + i)
+        mix[pl.ds(i, 1), :] = both(6 + i)
+    if fold:
+        odd = lax.axis_index("group") & 1
+
+        @pl.when(odd == 1)
+        def _():
+            for i in range(2):
+                mix[pl.ds(i, 1), :] = other[pl.ds(9 - i, 1), :]
+
     chip[pl.ds(0, 1), :] = jnp.maximum(own[...], both(0))
     chip[pl.ds(1, 1), :] = both(1)
 
@@ -147,19 +145,20 @@
                 pairs.append((b, a) if back else (a, b))
         return lax.ppermute(x, ("group", "blk"), pairs)
 
+    meta = pl.pallas_call(
+        meta_kernel,
+        out_shape=jax.ShapeDtypeStruct((META, LANES), jnp.bfloat16),
+        in_specs=[pl.BlockSpec(memory_space=pltpu.VMEM)] * 2,
+        out_specs=pl.BlockSpec(memory_space=pltpu.VMEM),
+        compiler_params=pltpu.CompilerParams(vmem_limit_bytes=4 * 2**20),
+    )(cluster.reshape(1, rows), doc_index.reshape(1, rows))
     block = pl.pallas_call(
         pack_kernel,
         out_shape=jax.ShapeDtypeStruct((width + META, LANES), jnp.bfloat16),
-        in_specs=[pl.BlockSpec(memory_space=pltpu.HBM)] * 3,
-        out_specs=pl.BlockSpec(memory_space=pltpu.VMEM),
-        scratch_shapes=[
-            pltpu.VMEM((rows, width), embedding.dtype),
-            pltpu.VMEM((1, rows), jnp.int32),
-            pltpu.VMEM((1, rows), jnp.int32),
-            pltpu.SemaphoreType.DMA((3,)),
-        ],
+        in_specs=[pl.BlockSpec(memory_space=pltpu.VMEM)] * 2,
+        out_specs=pl.BlockSpec(memory_space=pltpu.VMEM),
         compiler_params=pltpu.CompilerParams(vmem_limit_bytes=16 * 2**20),
-    )(embedding, cluster.reshape(1, rows), doc_index.reshape(1, rows))
+    )(embedding, meta)
 
     mate = swap(block)
     near = turn(block, 2, 4)
@@ -175,29 +174,27 @@
         places = places + [p + bit for p in places]
         bit *= 2
 
-    (own_best,) = score(1, block, keys, places, False)
-    rows_back, cols = [], None
-    for number, visitor in enumerate(visitors):
-        row_best, col_best = score(2, visitor, keys, places, True)
-        rows_back.append(row_best)
-        cols = col_best if cols is None else jnp.maximum(cols, col_best)
+    own_best = score(1, block, keys, places, False)
+    results = [score(2, visitor, keys, places, True) for visitor in visitors]
+    res = results[0]
+    for result in results[1:]:
+        res = jnp.maximum(res, result)
 
     bit = groups // 2
     while bit > 4:
-        cols = jnp.maximum(cols[:bit], turn(cols[bit:], bit, bit))
+        far_cols = turn(res[bit : 2 * bit], bit, bit)
+        res = jnp.concatenate([jnp.maximum(res[:bit], far_cols), res[2 * bit :]])
         bit //= 2
 
     fold = rounds == 1
-    odd = (lax.axis_index("group") & 1).astype(jnp.int32).reshape(1)
     small = jax.ShapeDtypeStruct((2, LANES), jnp.float32)
     near_out, mix_out, chip = pl.pallas_call(
         functools.partial(merge_kernel, fold),
         out_shape=[small] * 3,
-        in_specs=[pl.BlockSpec(memory_space=pltpu.VMEM)] * 4
-        + [pl.BlockSpec(memory_space=pltpu.SMEM)],
+        in_specs=[pl.BlockSpec(memory_space=pltpu.VMEM)] * 3,
         out_specs=[pl.BlockSpec(memory_space=pltpu.VMEM)] * 3,
         compiler_params=pltpu.CompilerParams(vmem_limit_bytes=4 * 2**20),
-    )(cols, swap(cols), swap(rows_back[0]), own_best, odd)
+    )(res, swap(res), own_best)
     chip = jnp.maximum(chip, turn(near_out, 2, 4))
     pairs = []
     for g in range(groups):
@@ -208,8 +205,8 @@
                 pairs.append((g * blks + i, (g ^ 6) * blks + i))
     chip = jnp.maximum(chip, lax.ppermute(mix_out, ("group", "blk"), pairs))
     if not fold:
-        for number, row_best in enumerate(rows_back):
-            chip = jnp.maximum(chip, visit(row_best, number, True))
+        for number, result in enumerate(results):
+            chip = jnp.maximum(chip, visit(result[groups : groups + 2], number, True))
     return jnp.maximum(chip[0], swap(chip[1]))
 
 

time: 30.3 us -> 30 us (0.990)
  starting transfers between devices: 13.9 us -> 13.4 us
    ppermute x7 -> x6, starting transfers between devices: 1.66 us -> 1.16 us  [swap(): return lax.ppermute(x, 'group', [(g, g ^ 1) for g in range(groups)])]
    ppermute x7 -> x6, waiting for transfers between devices: 1.12 us -> 1.36 us  [swap(): return lax.ppermute(x, 'group', [(g, g ^ 1) for g in range(groups)])]
  transfers between devices with their start and end apart: 13 -> 12, of which waited for: 5 -> 6; matrix products, arithmetic and copies ran while one was open for 0% -> 0% of each run, Pallas kernels for 3% -> 3%
where the time goes in v4:
time: 30 us; the launch traced here: 29.8 us
  starting transfers between devices  13.4 us (45%)
  waiting for transfers between devices  12.3 us (41%)
  Pallas kernels  2 us (7%)
  local copies, waits for them, and re-layouts  1.63 us (5%)
  other arithmetic  0.52 us (2%)
    ppermute x4, waiting for transfers between devices, turn(): lax.ppermute(x, 'group', [(g, g ^ (odd if g & 1 else even)) for g in rang...  7.41 us
    ppermute x4, starting transfers between devices, turn(): lax.ppermute(x, 'group', [(g, g ^ (odd if g & 1 else even)) for g in rang...  6.11 us
    ppermute x1, starting transfers between devices, visit(): return lax.ppermute(x, ('group', 'blk'), pairs)  3.65 us
    ppermute x1, starting transfers between devices, program(): chip = jnp.maximum(chip, lax.ppermute(mix_out, ('group', 'blk'), pairs))  2.46 us
    ppermute x1, waiting for transfers between devices, visit(): return lax.ppermute(x, ('group', 'blk'), pairs)  1.99 us
    pallas_call x2, Pallas kernels, score(): pl.pallas_call(functools.partial(score_kernel, count, places, cross), out...  1.81 us
    unnamed x6, local copies, waits for them, and re-layouts  1.62 us
    ppermute x1, waiting for transfers between devices, program(): chip = jnp.maximum(chip, lax.ppermute(mix_out, ('group', 'blk'), pairs))  1.49 us
  transfers between devices with their start and end apart: 12, of which 6 were waited for; matrix products, arithmetic and copies ran while one was open for 0% of the time, Pallas kernels for 3%

profile of v4, /device:TPU:0, one launch (start us, length us, event | category | flops | bytes accessed | tf_op | source)
XLA Modules:
  0.0 29.8 jit_solution(17080184711198528093)
XLA Ops:
  0.0 0.0 copy-start.1
  0.0 0.0 copy-start.2
  0.0 0.7 %copy-done.1 = s32[128]{0:T(128)S(1)} copy-done((s32[128]{0:T(128)S(1)}, s32[128]{0:T(128)}, u32[]{:S(2)}) %copy-start.1) | copy-done | bytes 536
  0.7 0.0 copy-done.2
  0.7 0.0 copy-start
  0.7 0.9 %copy-done = bf16[128,1024]{1,0:T(8,128)(2,1)S(1)} copy-done((bf16[128,1024]{1,0:T(8,128)(2,1)S(1)}, bf16[128,1024]{1,0:T(8,128)(2,1)}, u32[]{:S(2)}) %copy-start) | copy-done | bytes 262168
  1.6 0.1 shard_map.38.block.refs_1_.refs_0_
  1.8 0.5 %collective-permute-start = (bf16[1040,128]{1,0:T(8,128)(2,1)S(1)}, bf16[1040,128]{1,0:T(8,128)(2,1)S(1)}, u32[]{:S(2)}, u32[]{:S(2)}) collective-permute-start(bf16[1040,128]{1,0:T(8,128)(2,1)S(1)} %shard_map.38.block.refs_1_.refs_0_), channel_id=1, source_target_pairs={{0,4},{4,0},{8,12},{12,8},{16,20},{20,16},{24,28},{28,24},{1,5},{5... | collective-permute-start | bytes 798728 | tf_op jit(solution)/shard_map/ppermute | solution.py:130
  2.3 2.6 %collective-permute-start.2 = (bf16[1040,128]{1,0:T(8,128)(2,1)S(1)}, bf16[1040,128]{1,0:T(8,128)(2,1)S(1)}, u32[]{:S(2)}, u32[]{:S(2)}) collective-permute-start(bf16[1040,128]{1,0:T(8,128)(2,1)S(1)} %shard_map.38.block.refs_1_.refs_0_), channel_id=1, source_target_pairs={{0,8},{4,20},{8,0},{12,28},{16,24},{20,4},{24,16},{28,12},{1,9},{5... | collective-permute-start | bytes 798728 | tf_op jit(solution)/shard_map/ppermute | solution.py:133
  4.9 0.0 collective-permute-done.mate.refs_2_
  4.9 3.7 %collective-permute-start.1 = (bf16[2080,128]{1,0:T(8,128)(2,1)S(1)}, bf16[2080,128]{1,0:T(8,128)(2,1)S(1)}, u32[]{:S(2)}, u32[]{:S(2)}) collective-permute-start(bf16[2080,128]{1,0:T(8,128)(2,1)S(1)} %shard_map.39), channel_id=1, source_target_pairs={{0,3},{3,1},{1,2},{2,0},{4,5},{7,6},{5,4},{6,7},{8,11},{11,9},{9,1... | collective-permute-start | bytes 1597448 | tf_op jit(solution)/shard_map/ppermute | solution.py:146
  8.6 1.5 %collective-permute-start.3 = (bf16[1040,128]{1,0:T(8,128)(2,1)S(1)}, bf16[1040,128]{1,0:T(8,128)(2,1)S(1)}, u32[]{:S(2)}, u32[]{:S(2)}) collective-permute-start(bf16[1040,128]{1,0:T(8,128)(2,1)S(1)} %collective-permute-done.mate.refs_2_), channel_id=1, source_target_pairs={{0,8},{4,20},{8,0},{12,28},{16,24},{20,4},{24,16},{28,12},{1,9},{5... | collective-permute-start | bytes 798728 | tf_op jit(solution)/shard_map/ppermute | solution.py:133
  10.0 0.0 collective-permute-done.2.refs_3_
  10.0 1.5 %collective-permute-start.6 = (bf16[1040,128]{1,0:T(8,128)(2,1)S(1)}, bf16[1040,128]{1,0:T(8,128)(2,1)S(1)}, u32[]{:S(2)}, u32[]{:S(2)}) collective-permute-start(bf16[1040,128]{1,0:T(8,128)(2,1)S(1)} %collective-permute-done.2.refs_3_), channel_id=1, source_target_pairs={{0,16},{4,12},{8,24},{12,4},{16,0},{20,28},{24,8},{28,20},{1,17},{... | collective-permute-start | bytes 798728 | tf_op jit(solution)/shard_map/ppermute | solution.py:133
  11.5 0.0 collective-permute-start.5
  11.5 5.9 %collective-permute-done.3.refs_4_ = bf16[1040,128]{1,0:T(8,128)(2,1)S(1)} collective-permute-done((bf16[1040,128]{1,0:T(8,128)(2,1)S(1)}, bf16[1040,128]{1,0:T(8,128)(2,1)S(1)}, u32[]{:S(2)}, u32[]{:S(2)}) %collective-permute-start.3) | collective-permute-done | bytes 266272 | tf_op jit(solution)/shard_map/ppermute | solution.py:133
  17.4 0.0 collective-permute-start.4
  17.4 0.0 collective-permute-done.6.refs_7_
  17.4 0.5 %collective-permute-start.7 = (bf16[1040,128]{1,0:T(8,128)(2,1)S(1)}, bf16[1040,128]{1,0:T(8,128)(2,1)S(1)}, u32[]{:S(2)}, u32[]{:S(2)}) collective-permute-start(bf16[1040,128]{1,0:T(8,128)(2,1)S(1)} %collective-permute-done.6.refs_7_), channel_id=1, source_target_pairs={{0,4},{4,0},{8,12},{12,8},{16,20},{20,16},{24,28},{28,24},{1,5},{5... | collective-permute-start | bytes 798728 | tf_op jit(solution)/shard_map/ppermute | solution.py:130
  17.9 0.0 collective-permute-done.5.refs_6_
  18.0 2.0 %collective-permute-done.1.refs_0_ = bf16[2080,128]{1,0:T(8,128)(2,1)S(1)} collective-permute-done((bf16[2080,128]{1,0:T(8,128)(2,1)S(1)}, bf16[2080,128]{1,0:T(8,128)(2,1)S(1)}, u32[]{:S(2)}, u32[]{:S(2)}) %collective-permute-start.1) | collective-permute-done | bytes 532512 | tf_op jit(solution)/shard_map/ppermute | solution.py:146
  19.9 0.0 collective-permute-done.4.refs_5_
  19.9 0.0 collective-permute-done.7.refs_8_
  19.9 0.9 %shard_map.40.res = f32[10,128]{1,0:T(8,128)S(1)} custom-call(bf16[2080,128]{1,0:T(8,128)(2,1)S(1)} %collective-permute-done.1.refs_0_, bf16[1040,128]{1,0:T(8,128)(2,1)S(1)} %shard_map.38.block.refs_1_.refs_0_, bf16[1040,128]{1,0:T(8,128)(2,1)S(1)} %collective-permute-done.mate.refs_2_, bf16[1040,128]{1,0:T(8,128)(2,1)S(1)} %collective-permute-done.2.refs_3_, ...), custom_call_target="tpu_custom_call" | custom-call | flops 536870912 | bytes 2621440 | tf_op jit(solution)/shard_map/pallas_call | solution.py:92
  20.9 0.1 collective-permute-start.8
  20.9 0.9 %shard_map.41.own = f32[1,128]{1,0:T(1,128)S(1)} custom-call(bf16[1040,128]{1,0:T(8,128)(2,1)S(1)} %shard_map.38.block.refs_1_.refs_0_, bf16[1040,128]{1,0:T(8,128)(2,1)S(1)} %shard_map.38.block.refs_1_.refs_0_, bf16[1040,128]{1,0:T(8,128)(2,1)S(1)} %collective-permute-done.mate.refs_2_, bf16[1040,128]{1,0:T(8,128)(2,1)S(1)} %collective-permute-done.2.refs_3_, ...), custom_call_target="tpu_custom_call" | custom-call | flops 268435456 | bytes 2359296 | tf_op jit(solution)/shard_map/pallas_call | solution.py:92
  21.9 0.2 collective-permute-done.8.other
  22.1 2.5 %collective-permute-start.10 = (f32[2,128]{1,0:T(2,128)S(1)}, f32[2,128]{1,0:T(2,128)S(1)}, u32[]{:S(2)}, u32[]{:S(2)}) collective-permute-start(f32[2,128]{1,0:T(2,128)S(1)} %get-tuple-element.10), channel_id=1, source_target_pairs={{0,24},{1,25},{2,26},{3,27},{7,4},{5,7},{6,5},{4,6},{8,16},{9,17},... | collective-permute-start | bytes 3080 | tf_op jit(solution)/shard_map/ppermute | solution.py:206
  24.6 0.6 %collective-permute-start.9 = (f32[2,128]{1,0:T(2,128)S(1)}, f32[2,128]{1,0:T(2,128)S(1)}, u32[]{:S(2)}, u32[]{:S(2)}) collective-permute-start(f32[2,128]{1,0:T(2,128)S(1)} %get-tuple-element.9), channel_id=1, source_target_pairs={{0,8},{4,20},{8,0},{12,28},{16,24},{20,4},{24,16},{28,12},{1,9},{5... | collective-permute-start | bytes 3080 | tf_op jit(solution)/shard_map/ppermute | solution.py:133
  25.1 1.5 %collective-permute-done.10 = f32[2,128]{1,0:T(2,128)S(1)} collective-permute-done((f32[2,128]{1,0:T(2,128)S(1)}, f32[2,128]{1,0:T(2,128)S(1)}, u32[]{:S(2)}, u32[]{:S(2)}) %collective-permute-start.10) | collective-permute-done | bytes 1056 | tf_op jit(solution)/shard_map/ppermute | solution.py:206
  26.6 1.5 %collective-permute-done.9 = f32[2,128]{1,0:T(2,128)S(1)} collective-permute-done((f32[2,128]{1,0:T(2,128)S(1)}, f32[2,128]{1,0:T(2,128)S(1)}, u32[]{:S(2)}, u32[]{:S(2)}) %collective-permute-start.9) | collective-permute-done | bytes 1056 | tf_op jit(solution)/shard_map/ppermute | solution.py:133
  28.2 0.1 collective-permute-start.11
  28.2 1.1 %collective-permute-done.11 = f32[128]{0:T(128)S(1)} collective-permute-done((f32[128]{0:T(128)S(1)}, f32[128]{0:T(128)S(1)}, u32[]{:S(2)}, u32[]{:S(2)}) %collective-permute-start.11) | collective-permute-done | bytes 544 | tf_op jit(solution)/shard_map/ppermute | solution.py:130
  29.3 0.5 %bitcast_maximum_fusion = f32[128]{0:T(128)} fusion(f32[128]{0:T(128)S(1)} %collective-permute-done.11, f32[2,128]{1,0:T(2,128)S(1)} %maximum_maximum_fusion), kind=kLoop, calls=%fused_computation.1 | loop fusion | flops 128 | bytes 1536 | tf_op jit(solution)/shard_map/max | solution.py:210
  (5 shorter events, 0.1 us)
Async XLA Ops:
  0.0 0.7 %copy-start.1 = (s32[128]{0:T(128)S(1)}, s32[128]{0:T(128)}, u32[]{:S(2)}) copy-start(s32[128]{0:T(128)} %param.4) | copy-start | bytes 1540
  0.0 0.7 %copy-start.2 = (s32[128]{0:T(128)S(1)}, s32[128]{0:T(128)}, u32[]{:S(2)}) copy-start(s32[128]{0:T(128)} %param.5) | copy-start | bytes 1540
  0.7 0.9 %copy-start = (bf16[128,1024]{1,0:T(8,128)(2,1)S(1)}, bf16[128,1024]{1,0:T(8,128)(2,1)}, u32[]{:S(2)}) copy-start(bf16[128,1024]{1,0:T(8,128)(2,1)} %emb.1) | copy-start | bytes 786436
  1.8 3.1 %collective-permute-start = (bf16[1040,128]{1,0:T(8,128)(2,1)S(1)}, bf16[1040,128]{1,0:T(8,128)(2,1)S(1)}, u32[]{:S(2)}, u32[]{:S(2)}) collective-permute-start(bf16[1040,128]{1,0:T(8,128)(2,1)S(1)} %shard_map.38.block.refs_1_.refs_0_), channel_id=1, source_target_pairs={{0,4},{4,0},{8,12},{12,8},{16,20},{20,16},{24,28},{28,24},{1,5},{5... | collective-permute-start | bytes 798728 | tf_op jit(solution)/shard_map/ppermute | solution.py:130
  2.3 7.7 %collective-permute-start.2 = (bf16[1040,128]{1,0:T(8,128)(2,1)S(1)}, bf16[1040,128]{1,0:T(8,128)(2,1)S(1)}, u32[]{:S(2)}, u32[]{:S(2)}) collective-permute-start(bf16[1040,128]{1,0:T(8,128)(2,1)S(1)} %shard_map.38.block.refs_1_.refs_0_), channel_id=1, source_target_pairs={{0,8},{4,20},{8,0},{12,28},{16,24},{20,4},{24,16},{28,12},{1,9},{5... | collective-permute-start | bytes 798728 | tf_op jit(solution)/shard_map/ppermute | solution.py:133
  4.9 15.0 %collective-permute-start.1 = (bf16[2080,128]{1,0:T(8,128)(2,1)S(1)}, bf16[2080,128]{1,0:T(8,128)(2,1)S(1)}, u32[]{:S(2)}, u32[]{:S(2)}) collective-permute-start(bf16[2080,128]{1,0:T(8,128)(2,1)S(1)} %shard_map.39), channel_id=1, source_target_pairs={{0,3},{3,1},{1,2},{2,0},{4,5},{7,6},{5,4},{6,7},{8,11},{11,9},{9,1... | collective-permute-start | bytes 1597448 | tf_op jit(solution)/shard_map/ppermute | solution.py:146
  8.6 8.9 %collective-permute-start.3 = (bf16[1040,128]{1,0:T(8,128)(2,1)S(1)}, bf16[1040,128]{1,0:T(8,128)(2,1)S(1)}, u32[]{:S(2)}, u32[]{:S(2)}) collective-permute-start(bf16[1040,128]{1,0:T(8,128)(2,1)S(1)} %collective-permute-done.mate.refs_2_), channel_id=1, source_target_pairs={{0,8},{4,20},{8,0},{12,28},{16,24},{20,4},{24,16},{28,12},{1,9},{5... | collective-permute-start | bytes 798728 | tf_op jit(solution)/shard_map/ppermute | solution.py:133
  10.0 7.4 %collective-permute-start.6 = (bf16[1040,128]{1,0:T(8,128)(2,1)S(1)}, bf16[1040,128]{1,0:T(8,128)(2,1)S(1)}, u32[]{:S(2)}, u32[]{:S(2)}) collective-permute-start(bf16[1040,128]{1,0:T(8,128)(2,1)S(1)} %collective-permute-done.2.refs_3_), channel_id=1, source_target_pairs={{0,16},{4,12},{8,24},{12,4},{16,0},{20,28},{24,8},{28,20},{1,17},{... | collective-permute-start | bytes 798728 | tf_op jit(solution)/shard_map/ppermute | solution.py:133
  11.5 6.4 %collective-permute-start.5 = (bf16[1040,128]{1,0:T(8,128)(2,1)S(1)}, bf16[1040,128]{1,0:T(8,128)(2,1)S(1)}, u32[]{:S(2)}, u32[]{:S(2)}) collective-permute-start(bf16[1040,128]{1,0:T(8,128)(2,1)S(1)} %collective-permute-done.2.refs_3_), channel_id=1, source_target_pairs={{0,4},{4,0},{8,12},{12,8},{16,20},{20,16},{24,28},{28,24},{1,5},{5... | collective-permute-start | bytes 798728 | tf_op jit(solution)/shard_map/ppermute | solution.py:130
  17.4 2.5 %collective-permute-start.4 = (bf16[1040,128]{1,0:T(8,128)(2,1)S(1)}, bf16[1040,128]{1,0:T(8,128)(2,1)S(1)}, u32[]{:S(2)}, u32[]{:S(2)}) collective-permute-start(bf16[1040,128]{1,0:T(8,128)(2,1)S(1)} %collective-permute-done.3.refs_4_), channel_id=1, source_target_pairs={{0,4},{4,0},{8,12},{12,8},{16,20},{20,16},{24,28},{28,24},{1,5},{5... | collective-permute-start | bytes 798728 | tf_op jit(solution)/shard_map/ppermute | solution.py:130
  17.4 2.5 %collective-permute-start.7 = (bf16[1040,128]{1,0:T(8,128)(2,1)S(1)}, bf16[1040,128]{1,0:T(8,128)(2,1)S(1)}, u32[]{:S(2)}, u32[]{:S(2)}) collective-permute-start(bf16[1040,128]{1,0:T(8,128)(2,1)S(1)} %collective-permute-done.6.refs_7_), channel_id=1, source_target_pairs={{0,4},{4,0},{8,12},{12,8},{16,20},{20,16},{24,28},{28,24},{1,5},{5... | collective-permute-start | bytes 798728 | tf_op jit(solution)/shard_map/ppermute | solution.py:130
  20.9 1.2 %collective-permute-start.8 = (f32[10,128]{1,0:T(8,128)S(1)}, f32[10,128]{1,0:T(8,128)S(1)}, u32[]{:S(2)}, u32[]{:S(2)}) collective-permute-start(f32[10,128]{1,0:T(8,128)S(1)} %shard_map.40.res), channel_id=1, source_target_pairs={{0,4},{4,0},{8,12},{12,8},{16,20},{20,16},{24,28},{28,24},{1,5},{5... | collective-permute-start | bytes 15368 | tf_op jit(solution)/shard_map/ppermute | solution.py:130
  22.1 4.5 %collective-permute-start.10 = (f32[2,128]{1,0:T(2,128)S(1)}, f32[2,128]{1,0:T(2,128)S(1)}, u32[]{:S(2)}, u32[]{:S(2)}) collective-permute-start(f32[2,128]{1,0:T(2,128)S(1)} %get-tuple-element.10), channel_id=1, source_target_pairs={{0,24},{1,25},{2,26},{3,27},{7,4},{5,7},{6,5},{4,6},{8,16},{9,17},... | collective-permute-start | bytes 3080 | tf_op jit(solution)/shard_map/ppermute | solution.py:206
  24.6 3.6 %collective-permute-start.9 = (f32[2,128]{1,0:T(2,128)S(1)}, f32[2,128]{1,0:T(2,128)S(1)}, u32[]{:S(2)}, u32[]{:S(2)}) collective-permute-start(f32[2,128]{1,0:T(2,128)S(1)} %get-tuple-element.9), channel_id=1, source_target_pairs={{0,8},{4,20},{8,0},{12,28},{16,24},{20,4},{24,16},{28,12},{1,9},{5... | collective-permute-start | bytes 3080 | tf_op jit(solution)/shard_map/ppermute | solution.py:133
  28.2 1.2 %collective-permute-start.11 = (f32[128]{0:T(128)S(1)}, f32[128]{0:T(128)S(1)}, u32[]{:S(2)}, u32[]{:S(2)}) collective-permute-start(f32[128]{0:T(128)S(1)} %slice_bitcast_fusion), channel_id=1, source_target_pairs={{0,4},{4,0},{8,12},{12,8},{16,20},{20,16},{24,28},{28,24},{1,5},{5... | collective-permute-start | bytes 1544 | tf_op jit(solution)/shard_map/ppermute | solution.py:130

commit v5 on v4

--- a/solution.py
+++ b/solution.py
@@ -103,13 +103,14 @@
     )(query, *keys)
 
 
-def merge_kernel(fold, res, other, own, near, mix, chip):
+def merge_kernel(fold, res, other, near, side, mix, home):
     def both(p):
         q = (p & ~6 | (p & 2) << 1 | (p & 4) >> 1) ^ 1
         return jnp.maximum(res[pl.ds(p, 1), :], other[pl.ds(q, 1), :])
 
+    near[...] = both(2)
+    side[...] = both(4)
     for i in range(2):
-        near[pl.ds(i, 1), :] = both(2 + i)
         mix[pl.ds(i, 1), :] = both(6 + i)
     if fold:
         odd = lax.axis_index("group") & 1
@@ -119,8 +120,7 @@
             for i in range(2):
                 mix[pl.ds(i, 1), :] = other[pl.ds(9 - i, 1), :]
 
-    chip[pl.ds(0, 1), :] = jnp.maximum(own[...], both(0))
-    chip[pl.ds(1, 1), :] = both(1)
+    home[...] = both(0)
 
 
 def program(groups, blks, embedding, cluster, doc_index):
@@ -187,15 +187,15 @@
         bit //= 2
 
     fold = rounds == 1
-    small = jax.ShapeDtypeStruct((2, LANES), jnp.float32)
-    near_out, mix_out, chip = pl.pallas_call(
+    one = jax.ShapeDtypeStruct((1, LANES), jnp.float32)
+    two = jax.ShapeDtypeStruct((2, LANES), jnp.float32)
+    near_out, side_out, mix_out, home = pl.pallas_call(
         functools.partial(merge_kernel, fold),
-        out_shape=[small] * 3,
-        in_specs=[pl.BlockSpec(memory_space=pltpu.VMEM)] * 3,
-        out_specs=[pl.BlockSpec(memory_space=pltpu.VMEM)] * 3,
+        out_shape=[one, one, two, one],
+        in_specs=[pl.BlockSpec(memory_space=pltpu.VMEM)] * 2,
+        out_specs=[pl.BlockSpec(memory_space=pltpu.VMEM)] * 4,
         compiler_params=pltpu.CompilerParams(vmem_limit_bytes=4 * 2**20),
-    )(res, swap(res), own_best)
-    chip = jnp.maximum(chip, turn(near_out, 2, 4))
+    )(res, swap(res))
     pairs = []
     for g in range(groups):
         for i in range(blks):
@@ -203,11 +203,13 @@
                 pairs.append((g * blks + order[(i + 1) % blks], g * blks + order[i]))
             else:
                 pairs.append((g * blks + i, (g ^ 6) * blks + i))
-    chip = jnp.maximum(chip, lax.ppermute(mix_out, ("group", "blk"), pairs))
+    mixed = lax.ppermute(mix_out, ("group", "blk"), pairs)
+    best = jnp.maximum(jnp.maximum(home[0], own_best[0]), turn(near_out[0], 2, 4))
+    best = jnp.maximum(best, turn(side_out[0], 4, 2))
     if not fold:
         for number, result in enumerate(results):
-            chip = jnp.maximum(chip, visit(result[groups : groups + 2], number, True))
-    return jnp.maximum(chip[0], swap(chip[1]))
+            mixed = jnp.maximum(mixed, visit(result[groups : groups + 2], number, True))
+    return jnp.maximum(jnp.maximum(best, mixed[0]), swap(mixed[1]))
 
 
 def solution(mesh):

time: 30 us -> 29.3 us (0.977)
  waiting for transfers between devices: 12.3 us -> 10.7 us
  starting transfers between devices: 13.4 us -> 14.2 us
    ppermute x4 -> x5, waiting for transfers between devices: 7.41 us -> 6.58 us  [turn(): lax.ppermute(x, 'group', [(g, g ^ (odd if g & 1 else even)) for g in rang...]
    ppermute x1, waiting for transfers between devices: 1.49 us -> 0.98 us  [program(): mixed = lax.ppermute(mix_out, ('group', 'blk'), pairs)]
    ppermute x4 -> x5, starting transfers between devices: 6.11 us -> 6.62 us  [turn(): lax.ppermute(x, 'group', [(g, g ^ (odd if g & 1 else even)) for g in rang...]
    ppermute x6, starting transfers between devices: 1.16 us -> 1.52 us  [swap(): return lax.ppermute(x, 'group', [(g, g ^ 1) for g in range(groups)])]
  transfers between devices with their start and end apart: 12 -> 13, of which waited for: 6 -> 6; matrix products, arithmetic and copies ran while one was open for 0% -> 0% of each run, Pallas kernels for 3% -> 3%
where the time goes in v5:
time: 29.3 us; the launch traced here: 29.1 us
  starting transfers between devices  14.2 us (48%)
  waiting for transfers between devices  10.7 us (37%)
  Pallas kernels  1.99 us (7%)
  local copies, waits for them, and re-layouts  1.62 us (6%)
  other arithmetic  0.52 us (2%)
    ppermute x5, starting transfers between devices, turn(): lax.ppermute(x, 'group', [(g, g ^ (odd if g & 1 else even)) for g in rang...  6.62 us
    ppermute x5, waiting for transfers between devices, turn(): lax.ppermute(x, 'group', [(g, g ^ (odd if g & 1 else even)) for g in rang...  6.58 us
    ppermute x1, starting transfers between devices, visit(): return lax.ppermute(x, ('group', 'blk'), pairs)  3.65 us
    ppermute x1, starting transfers between devices, program(): mixed = lax.ppermute(mix_out, ('group', 'blk'), pairs)  2.41 us
    ppermute x1, waiting for transfers between devices, visit(): return lax.ppermute(x, ('group', 'blk'), pairs)  1.99 us
    pallas_call x2, Pallas kernels, score(): pl.pallas_call(functools.partial(score_kernel, count, places, cross), out...  1.8 us
    unnamed x6, local copies, waits for them, and re-layouts  1.62 us
    ppermute x6, starting transfers between devices, swap(): return lax.ppermute(x, 'group', [(g, g ^ 1) for g in range(groups)])  1.52 us
  transfers between devices with their start and end apart: 13, of which 6 were waited for; matrix products, arithmetic and copies ran while one was open for 0% of the time, Pallas kernels for 3%

profile of v5, /device:TPU:0, one launch (start us, length us, event | category | flops | bytes accessed | tf_op | source)
XLA Modules:
  0.0 29.1 jit_solution(9315517694669684396)
XLA Ops:
  0.0 0.0 copy-start.1
  0.0 0.0 copy-start.2
  0.0 0.7 %copy-done.1 = s32[128]{0:T(128)S(1)} copy-done((s32[128]{0:T(128)S(1)}, s32[128]{0:T(128)}, u32[]{:S(2)}) %copy-start.1) | copy-done | bytes 536
  0.7 0.0 copy-done.2
  0.7 0.0 copy-start
  0.7 0.9 %copy-done = bf16[128,1024]{1,0:T(8,128)(2,1)S(1)} copy-done((bf16[128,1024]{1,0:T(8,128)(2,1)S(1)}, bf16[128,1024]{1,0:T(8,128)(2,1)}, u32[]{:S(2)}) %copy-start) | copy-done | bytes 262168
  1.6 0.1 shard_map.38.block.refs_1_.refs_0_
  1.8 0.5 %collective-permute-start = (bf16[1040,128]{1,0:T(8,128)(2,1)S(1)}, bf16[1040,128]{1,0:T(8,128)(2,1)S(1)}, u32[]{:S(2)}, u32[]{:S(2)}) collective-permute-start(bf16[1040,128]{1,0:T(8,128)(2,1)S(1)} %shard_map.38.block.refs_1_.refs_0_), channel_id=1, source_target_pairs={{0,4},{4,0},{8,12},{12,8},{16,20},{20,16},{24,28},{28,24},{1,5},{5... | collective-permute-start | bytes 798728 | tf_op jit(solution)/shard_map/ppermute | solution.py:130
  2.3 2.6 %collective-permute-start.2 = (bf16[1040,128]{1,0:T(8,128)(2,1)S(1)}, bf16[1040,128]{1,0:T(8,128)(2,1)S(1)}, u32[]{:S(2)}, u32[]{:S(2)}) collective-permute-start(bf16[1040,128]{1,0:T(8,128)(2,1)S(1)} %shard_map.38.block.refs_1_.refs_0_), channel_id=1, source_target_pairs={{0,8},{4,20},{8,0},{12,28},{16,24},{20,4},{24,16},{28,12},{1,9},{5... | collective-permute-start | bytes 798728 | tf_op jit(solution)/shard_map/ppermute | solution.py:133
  4.9 0.0 collective-permute-done.mate.refs_2_
  4.9 3.7 %collective-permute-start.1 = (bf16[2080,128]{1,0:T(8,128)(2,1)S(1)}, bf16[2080,128]{1,0:T(8,128)(2,1)S(1)}, u32[]{:S(2)}, u32[]{:S(2)}) collective-permute-start(bf16[2080,128]{1,0:T(8,128)(2,1)S(1)} %shard_map.39), channel_id=1, source_target_pairs={{0,3},{3,1},{1,2},{2,0},{4,5},{7,6},{5,4},{6,7},{8,11},{11,9},{9,1... | collective-permute-start | bytes 1597448 | tf_op jit(solution)/shard_map/ppermute | solution.py:146
  8.6 1.5 %collective-permute-start.3 = (bf16[1040,128]{1,0:T(8,128)(2,1)S(1)}, bf16[1040,128]{1,0:T(8,128)(2,1)S(1)}, u32[]{:S(2)}, u32[]{:S(2)}) collective-permute-start(bf16[1040,128]{1,0:T(8,128)(2,1)S(1)} %collective-permute-done.mate.refs_2_), channel_id=1, source_target_pairs={{0,8},{4,20},{8,0},{12,28},{16,24},{20,4},{24,16},{28,12},{1,9},{5... | collective-permute-start | bytes 798728 | tf_op jit(solution)/shard_map/ppermute | solution.py:133
  10.0 0.0 collective-permute-done.2.refs_3_
  10.0 1.5 %collective-permute-start.6 = (bf16[1040,128]{1,0:T(8,128)(2,1)S(1)}, bf16[1040,128]{1,0:T(8,128)(2,1)S(1)}, u32[]{:S(2)}, u32[]{:S(2)}) collective-permute-start(bf16[1040,128]{1,0:T(8,128)(2,1)S(1)} %collective-permute-done.2.refs_3_), channel_id=1, source_target_pairs={{0,16},{4,12},{8,24},{12,4},{16,0},{20,28},{24,8},{28,20},{1,17},{... | collective-permute-start | bytes 798728 | tf_op jit(solution)/shard_map/ppermute | solution.py:133
  11.5 0.0 collective-permute-start.5
  11.5 5.9 %collective-permute-done.3.refs_4_ = bf16[1040,128]{1,0:T(8,128)(2,1)S(1)} collective-permute-done((bf16[1040,128]{1,0:T(8,128)(2,1)S(1)}, bf16[1040,128]{1,0:T(8,128)(2,1)S(1)}, u32[]{:S(2)}, u32[]{:S(2)}) %collective-permute-start.3) | collective-permute-done | bytes 266272 | tf_op jit(solution)/shard_map/ppermute | solution.py:133
  17.4 0.0 collective-permute-start.4
  17.4 0.0 collective-permute-done.6.refs_7_
  17.4 0.5 %collective-permute-start.7 = (bf16[1040,128]{1,0:T(8,128)(2,1)S(1)}, bf16[1040,128]{1,0:T(8,128)(2,1)S(1)}, u32[]{:S(2)}, u32[]{:S(2)}) collective-permute-start(bf16[1040,128]{1,0:T(8,128)(2,1)S(1)} %collective-permute-done.6.refs_7_), channel_id=1, source_target_pairs={{0,4},{4,0},{8,12},{12,8},{16,20},{20,16},{24,28},{28,24},{1,5},{5... | collective-permute-start | bytes 798728 | tf_op jit(solution)/shard_map/ppermute | solution.py:130
  17.9 0.0 collective-permute-done.5.refs_6_
  18.0 2.0 %collective-permute-done.1.refs_0_ = bf16[2080,128]{1,0:T(8,128)(2,1)S(1)} collective-permute-done((bf16[2080,128]{1,0:T(8,128)(2,1)S(1)}, bf16[2080,128]{1,0:T(8,128)(2,1)S(1)}, u32[]{:S(2)}, u32[]{:S(2)}) %collective-permute-start.1) | collective-permute-done | bytes 532512 | tf_op jit(solution)/shard_map/ppermute | solution.py:146
  19.9 0.0 collective-permute-done.4.refs_5_
  19.9 0.0 collective-permute-done.7.refs_8_
  19.9 0.9 %shard_map.40.res = f32[10,128]{1,0:T(8,128)S(1)} custom-call(bf16[2080,128]{1,0:T(8,128)(2,1)S(1)} %collective-permute-done.1.refs_0_, bf16[1040,128]{1,0:T(8,128)(2,1)S(1)} %shard_map.38.block.refs_1_.refs_0_, bf16[1040,128]{1,0:T(8,128)(2,1)S(1)} %collective-permute-done.mate.refs_2_, bf16[1040,128]{1,0:T(8,128)(2,1)S(1)} %collective-permute-done.2.refs_3_, ...), custom_call_target="tpu_custom_call" | custom-call | flops 536870912 | bytes 2621440 | tf_op jit(solution)/shard_map/pallas_call | solution.py:92
  20.9 0.1 collective-permute-start.8
  20.9 1.2 %collective-permute-done.8.other = f32[10,128]{1,0:T(8,128)S(1)} collective-permute-done((f32[10,128]{1,0:T(8,128)S(1)}, f32[10,128]{1,0:T(8,128)S(1)}, u32[]{:S(2)}, u32[]{:S(2)}) %collective-permute-start.8) | collective-permute-done | bytes 5152 | tf_op jit(solution)/shard_map/ppermute | solution.py:130
  22.1 2.4 %collective-permute-start.11 = (f32[2,128]{1,0:T(2,128)S(1)}, f32[2,128]{1,0:T(2,128)S(1)}, u32[]{:S(2)}, u32[]{:S(2)}) collective-permute-start(f32[2,128]{1,0:T(2,128)S(1)} %get-tuple-element.12), channel_id=1, source_target_pairs={{0,24},{1,25},{2,26},{3,27},{7,4},{5,7},{6,5},{4,6},{8,16},{9,17},... | collective-permute-start | bytes 3080 | tf_op jit(solution)/shard_map/ppermute | solution.py:206
  24.5 0.5 %collective-permute-start.10 = (f32[128]{0:T(128)S(1)}, f32[128]{0:T(128)S(1)}, u32[]{:S(2)}, u32[]{:S(2)}) collective-permute-start(f32[128]{0:T(128)S(1)} %bitcast.19), channel_id=1, source_target_pairs={{0,16},{4,12},{8,24},{12,4},{16,0},{20,28},{24,8},{28,20},{1,17},{... | collective-permute-start | bytes 1544 | tf_op jit(solution)/shard_map/ppermute | solution.py:133
  25.0 0.6 %collective-permute-start.9 = (f32[128]{0:T(128)S(1)}, f32[128]{0:T(128)S(1)}, u32[]{:S(2)}, u32[]{:S(2)}) collective-permute-start(f32[128]{0:T(128)S(1)} %bitcast.18), channel_id=1, source_target_pairs={{0,8},{4,20},{8,0},{12,28},{16,24},{20,4},{24,16},{28,12},{1,9},{5... | collective-permute-start | bytes 1544 | tf_op jit(solution)/shard_map/ppermute | solution.py:133
  25.6 1.0 %collective-permute-done.11 = f32[2,128]{1,0:T(2,128)S(1)} collective-permute-done((f32[2,128]{1,0:T(2,128)S(1)}, f32[2,128]{1,0:T(2,128)S(1)}, u32[]{:S(2)}, u32[]{:S(2)}) %collective-permute-start.11) | collective-permute-done | bytes 1056 | tf_op jit(solution)/shard_map/ppermute | solution.py:206
  26.6 0.4 %collective-permute-start.12 = (f32[128]{0:T(128)S(1)}, f32[128]{0:T(128)S(1)}, u32[]{:S(2)}, u32[]{:S(2)}) collective-permute-start(f32[128]{0:T(128)S(1)} %slice_bitcast_fusion), channel_id=1, source_target_pairs={{0,4},{4,0},{8,12},{12,8},{16,20},{20,16},{24,28},{28,24},{1,5},{5... | collective-permute-start | bytes 1544 | tf_op jit(solution)/shard_map/ppermute | solution.py:130
  27.0 0.9 %shard_map.42 = f32[1,128]{1,0:T(1,128)S(1)} custom-call(bf16[1040,128]{1,0:T(8,128)(2,1)S(1)} %shard_map.38.block.refs_1_.refs_0_, bf16[1040,128]{1,0:T(8,128)(2,1)S(1)} %shard_map.38.block.refs_1_.refs_0_, bf16[1040,128]{1,0:T(8,128)(2,1)S(1)} %collective-permute-done.mate.refs_2_, bf16[1040,128]{1,0:T(8,128)(2,1)S(1)} %collective-permute-done.2.refs_3_, ...), custom_call_target="tpu_custom_call" | custom-call | flops 268435456 | bytes 2359296 | tf_op jit(solution)/shard_map/pallas_call | solution.py:92
  27.9 0.2 collective-permute-done.10
  28.1 0.5 %collective-permute-done.9 = f32[128]{0:T(128)S(1)} collective-permute-done((f32[128]{0:T(128)S(1)}, f32[128]{0:T(128)S(1)}, u32[]{:S(2)}, u32[]{:S(2)}) %collective-permute-start.9) | collective-permute-done | bytes 544 | tf_op jit(solution)/shard_map/ppermute | solution.py:133
  28.6 0.0 collective-permute-done.12
  28.6 0.5 %fusion = f32[128]{0:T(128)} fusion(f32[128]{0:T(128)S(1)} %collective-permute-done.12, f32[128]{0:T(128)S(1)} %collective-permute-done.10, f32[128]{0:T(128)S(1)} %collective-permute-done.9, f32[2,128]{1,0:T(2,128)S(1)} %collective-permute-done.11, f32[1,128]{1,0:T(1,128)S(1)} %get-tuple-element.9, f32[1,128]{1,0:T(1,128)S(1)} %shard_map.42), kind=kLoop, calls=%fused_computation.1 | loop fusion | flops 640 | bytes 3584 | tf_op jit(solution)/shard_map/max | solution.py:212
  (4 shorter events, 0.1 us)
Async XLA Ops:
  0.0 0.7 %copy-start.1 = (s32[128]{0:T(128)S(1)}, s32[128]{0:T(128)}, u32[]{:S(2)}) copy-start(s32[128]{0:T(128)} %param.4) | copy-start | bytes 1540
  0.0 0.7 %copy-start.2 = (s32[128]{0:T(128)S(1)}, s32[128]{0:T(128)}, u32[]{:S(2)}) copy-start(s32[128]{0:T(128)} %param.5) | copy-start | bytes 1540
  0.7 0.9 %copy-start = (bf16[128,1024]{1,0:T(8,128)(2,1)S(1)}, bf16[128,1024]{1,0:T(8,128)(2,1)}, u32[]{:S(2)}) copy-start(bf16[128,1024]{1,0:T(8,128)(2,1)} %emb.1) | copy-start | bytes 786436
  1.8 3.1 %collective-permute-start = (bf16[1040,128]{1,0:T(8,128)(2,1)S(1)}, bf16[1040,128]{1,0:T(8,128)(2,1)S(1)}, u32[]{:S(2)}, u32[]{:S(2)}) collective-permute-start(bf16[1040,128]{1,0:T(8,128)(2,1)S(1)} %shard_map.38.block.refs_1_.refs_0_), channel_id=1, source_target_pairs={{0,4},{4,0},{8,12},{12,8},{16,20},{20,16},{24,28},{28,24},{1,5},{5... | collective-permute-start | bytes 798728 | tf_op jit(solution)/shard_map/ppermute | solution.py:130
  2.3 7.7 %collective-permute-start.2 = (bf16[1040,128]{1,0:T(8,128)(2,1)S(1)}, bf16[1040,128]{1,0:T(8,128)(2,1)S(1)}, u32[]{:S(2)}, u32[]{:S(2)}) collective-permute-start(bf16[1040,128]{1,0:T(8,128)(2,1)S(1)} %shard_map.38.block.refs_1_.refs_0_), channel_id=1, source_target_pairs={{0,8},{4,20},{8,0},{12,28},{16,24},{20,4},{24,16},{28,12},{1,9},{5... | collective-permute-start | bytes 798728 | tf_op jit(solution)/shard_map/ppermute | solution.py:133
  4.9 15.0 %collective-permute-start.1 = (bf16[2080,128]{1,0:T(8,128)(2,1)S(1)}, bf16[2080,128]{1,0:T(8,128)(2,1)S(1)}, u32[]{:S(2)}, u32[]{:S(2)}) collective-permute-start(bf16[2080,128]{1,0:T(8,128)(2,1)S(1)} %shard_map.39), channel_id=1, source_target_pairs={{0,3},{3,1},{1,2},{2,0},{4,5},{7,6},{5,4},{6,7},{8,11},{11,9},{9,1... | collective-permute-start | bytes 1597448 | tf_op jit(solution)/shard_map/ppermute | solution.py:146
  8.6 8.9 %collective-permute-start.3 = (bf16[1040,128]{1,0:T(8,128)(2,1)S(1)}, bf16[1040,128]{1,0:T(8,128)(2,1)S(1)}, u32[]{:S(2)}, u32[]{:S(2)}) collective-permute-start(bf16[1040,128]{1,0:T(8,128)(2,1)S(1)} %collective-permute-done.mate.refs_2_), channel_id=1, source_target_pairs={{0,8},{4,20},{8,0},{12,28},{16,24},{20,4},{24,16},{28,12},{1,9},{5... | collective-permute-start | bytes 798728 | tf_op jit(solution)/shard_map/ppermute | solution.py:133
  10.0 7.4 %collective-permute-start.6 = (bf16[1040,128]{1,0:T(8,128)(2,1)S(1)}, bf16[1040,128]{1,0:T(8,128)(2,1)S(1)}, u32[]{:S(2)}, u32[]{:S(2)}) collective-permute-start(bf16[1040,128]{1,0:T(8,128)(2,1)S(1)} %collective-permute-done.2.refs_3_), channel_id=1, source_target_pairs={{0,16},{4,12},{8,24},{12,4},{16,0},{20,28},{24,8},{28,20},{1,17},{... | collective-permute-start | bytes 798728 | tf_op jit(solution)/shard_map/ppermute | solution.py:133
  11.5 6.4 %collective-permute-start.5 = (bf16[1040,128]{1,0:T(8,128)(2,1)S(1)}, bf16[1040,128]{1,0:T(8,128)(2,1)S(1)}, u32[]{:S(2)}, u32[]{:S(2)}) collective-permute-start(bf16[1040,128]{1,0:T(8,128)(2,1)S(1)} %collective-permute-done.2.refs_3_), channel_id=1, source_target_pairs={{0,4},{4,0},{8,12},{12,8},{16,20},{20,16},{24,28},{28,24},{1,5},{5... | collective-permute-start | bytes 798728 | tf_op jit(solution)/shard_map/ppermute | solution.py:130
  17.4 2.5 %collective-permute-start.4 = (bf16[1040,128]{1,0:T(8,128)(2,1)S(1)}, bf16[1040,128]{1,0:T(8,128)(2,1)S(1)}, u32[]{:S(2)}, u32[]{:S(2)}) collective-permute-start(bf16[1040,128]{1,0:T(8,128)(2,1)S(1)} %collective-permute-done.3.refs_4_), channel_id=1, source_target_pairs={{0,4},{4,0},{8,12},{12,8},{16,20},{20,16},{24,28},{28,24},{1,5},{5... | collective-permute-start | bytes 798728 | tf_op jit(solution)/shard_map/ppermute | solution.py:130
  17.4 2.5 %collective-permute-start.7 = (bf16[1040,128]{1,0:T(8,128)(2,1)S(1)}, bf16[1040,128]{1,0:T(8,128)(2,1)S(1)}, u32[]{:S(2)}, u32[]{:S(2)}) collective-permute-start(bf16[1040,128]{1,0:T(8,128)(2,1)S(1)} %collective-permute-done.6.refs_7_), channel_id=1, source_target_pairs={{0,4},{4,0},{8,12},{12,8},{16,20},{20,16},{24,28},{28,24},{1,5},{5... | collective-permute-start | bytes 798728 | tf_op jit(solution)/shard_map/ppermute | solution.py:130
  20.9 1.2 %collective-permute-start.8 = (f32[10,128]{1,0:T(8,128)S(1)}, f32[10,128]{1,0:T(8,128)S(1)}, u32[]{:S(2)}, u32[]{:S(2)}) collective-permute-start(f32[10,128]{1,0:T(8,128)S(1)} %shard_map.40.res), channel_id=1, source_target_pairs={{0,4},{4,0},{8,12},{12,8},{16,20},{20,16},{24,28},{28,24},{1,5},{5... | collective-permute-start | bytes 15368 | tf_op jit(solution)/shard_map/ppermute | solution.py:130
  22.1 4.5 %collective-permute-start.11 = (f32[2,128]{1,0:T(2,128)S(1)}, f32[2,128]{1,0:T(2,128)S(1)}, u32[]{:S(2)}, u32[]{:S(2)}) collective-permute-start(f32[2,128]{1,0:T(2,128)S(1)} %get-tuple-element.12), channel_id=1, source_target_pairs={{0,24},{1,25},{2,26},{3,27},{7,4},{5,7},{6,5},{4,6},{8,16},{9,17},... | collective-permute-start | bytes 3080 | tf_op jit(solution)/shard_map/ppermute | solution.py:206
  24.5 3.5 %collective-permute-start.10 = (f32[128]{0:T(128)S(1)}, f32[128]{0:T(128)S(1)}, u32[]{:S(2)}, u32[]{:S(2)}) collective-permute-start(f32[128]{0:T(128)S(1)} %bitcast.19), channel_id=1, source_target_pairs={{0,16},{4,12},{8,24},{12,4},{16,0},{20,28},{24,8},{28,20},{1,17},{... | collective-permute-start | bytes 1544 | tf_op jit(solution)/shard_map/ppermute | solution.py:133
  25.0 3.5 %collective-permute-start.9 = (f32[128]{0:T(128)S(1)}, f32[128]{0:T(128)S(1)}, u32[]{:S(2)}, u32[]{:S(2)}) collective-permute-start(f32[128]{0:T(128)S(1)} %bitcast.18), channel_id=1, source_target_pairs={{0,8},{4,20},{8,0},{12,28},{16,24},{20,4},{24,16},{28,12},{1,9},{5... | collective-permute-start | bytes 1544 | tf_op jit(solution)/shard_map/ppermute | solution.py:133
  26.6 2.0 %collective-permute-start.12 = (f32[128]{0:T(128)S(1)}, f32[128]{0:T(128)S(1)}, u32[]{:S(2)}, u32[]{:S(2)}) collective-permute-start(f32[128]{0:T(128)S(1)} %slice_bitcast_fusion), channel_id=1, source_target_pairs={{0,4},{4,0},{8,12},{12,8},{16,20},{20,16},{24,28},{28,24},{1,5},{5... | collective-permute-start | bytes 1544 | tf_op jit(solution)/shard_map/ppermute | solution.py:130
